TPU v7x, 512 devices: a whole 4x4x16 slice. The times are simulated.
512 devices in a mesh: kv: 32 (over z, core), mp: 16 (over y, x).
Axes of the slice: x: 4, y: 4, z: 16, core: 2. Of those that a mesh axis runs over, the one named last changes fastest.
Arguments:
- queries: bfloat16 [32, 8192], P(None, ('kv', 'mp')), may hold values from -200 to 200
- key_value_pages: bfloat16 [1024, 128, 8, 256], P('kv', 'mp'), may hold values from -12 to 12
- request_page_index: int32 [32, 32], replicated, may hold values from -1 to 1023, as said below
- lengths: int32 [32], replicated, may hold values from 1024 to 4096, as said below
- request_adapter_index: int32 [32], replicated, may hold values from 0 to 63
- output_weight: bfloat16 [8192, 8192], P('mp', 'kv'), may hold values from -0.5 to 0.5
- down_weight_columns: bfloat16 [8192, 1024], P('mp'), may hold values from -0.5 to 0.5
- up_weight_rows: bfloat16 [1024, 8192], P(None, 'kv'), may hold values from -0.75 to 0.75
Outputs:
- block_output: bfloat16 [32, 8192], P('mp', 'kv')
Inputs may be any that keep to these rules, and one draw needn't show every extreme that they name: `request_page_index`: row r holds the pages of request r in order: its first ceil(lengths[r] / 128) entries are pages of 0 to 1023, no page in two places, the others -1. Page p lies on index p // 32 of kv. `lengths`: some request has exactly 4096.
All inputs are finite; a program needn't handle non-finite values.
Results may differ from a plain program's by a relative error of at most 0.017.
Values may be sent and summed in bfloat16 or wider, within the bound.
No kernel may reach another device: no remote copies, remote signals or barrier semaphores. Data moves between devices by JAX's collectives and lax.ppermute only.
A program may use at most 64 MiB of HBM per device.

v0:
```python
import math

import jax
import jax.numpy as jnp
from jax import lax
from jax.sharding import PartitionSpec as P

ADAPTER_RANK = 16


NEG = -1e30
ADAPTER_SCALE = 2.0


def combined_all(value, axis, join):
    pieces = jax.tree.map(lambda part: lax.all_gather(part, axis), value)
    head = jax.tree.map(lambda part: part[0], pieces)
    tail = jax.tree.map(lambda part: part[1:], pieces)
    running, _ = lax.scan(lambda running, piece: (join(running, piece), None), head, tail)
    return running


def combine_parts(parts, axis):
    outputs, peaks, totals = parts
    peak = jnp.max(peaks, axis=axis)
    factor = jnp.exp(peaks - jnp.expand_dims(peak, axis))
    total = jnp.sum(factor * totals, axis=axis)
    output = jnp.sum(factor[..., None] * outputs, axis=axis)
    return (output, peak, total)


def merge_pair(first, second):
    peak = jnp.maximum(first[1], second[1])
    factor_a = jnp.exp(first[1] - peak)
    factor_b = jnp.exp(second[1] - peak)
    output = factor_a[..., None] * first[0] + factor_b[..., None] * second[0]
    return (output, peak, factor_a * first[2] + factor_b * second[2])


def combine_heads(parts):
    return combine_parts(parts, 1)


def on_device(
    queries,
    key_value_pages,
    request_page_index,
    lengths,
    request_adapter_index,
    output_weight,
    down_weight_columns,
    up_weight_rows,
):
    model_count = lax.axis_size("mp")
    whole_queries = lax.all_gather(queries, ("kv", "mp"), axis=1, tiled=True)
    requests = whole_queries.shape[0]
    pages_here = key_value_pages.shape[0]
    slice_tokens = key_value_pages.shape[1]
    kv_heads = key_value_pages.shape[2]
    head_size = key_value_pages.shape[3] // 2
    heads = whole_queries.shape[1] // head_size
    group = heads // kv_heads
    page_size = slice_tokens * model_count
    max_pages = request_page_index.shape[1]
    scale = 1.0 / math.sqrt(head_size)
    flat_pages = request_page_index.reshape(-1)
    request_of = jnp.repeat(jnp.arange(requests, dtype=jnp.int32), max_pages)
    slot_of = jnp.tile(jnp.arange(max_pages, dtype=jnp.int32), requests)
    local_ids = flat_pages - lax.axis_index("kv") * pages_here
    inside = (flat_pages >= 0) & (local_ids >= 0) & (local_ids < pages_here)
    target = jnp.where(inside, local_ids, pages_here)
    owner = jnp.full((pages_here,), -1, jnp.int32).at[target].set(request_of, mode="drop")
    position = jnp.zeros((pages_here,), jnp.int32).at[target].set(slot_of, mode="drop")
    safe_owner = jnp.maximum(owner, 0)
    first_token = position * page_size + lax.axis_index("mp") * slice_tokens
    token_place = first_token[:, None] + jnp.arange(slice_tokens, dtype=jnp.int32)[None, :]
    valid = (owner >= 0)[:, None] & (token_place < lengths[safe_owner][:, None])
    valid_full = valid[:, None, None, :]
    page_queries = whole_queries[safe_owner].reshape(pages_here, kv_heads, group, head_size)
    keys_here = key_value_pages[..., :head_size]
    values_here = key_value_pages[..., head_size:]
    scores = (
        jnp.einsum("pkgd,ptkd->pkgt", page_queries, keys_here, preferred_element_type=jnp.float32)
        * scale
    )
    scores = jnp.where(valid_full, scores, NEG)
    page_peak = jnp.max(scores, axis=-1)
    member = owner[:, None] == jnp.arange(requests, dtype=jnp.int32)[None, :]
    request_peak = jnp.max(jnp.where(member[:, :, None, None], page_peak[:, None], NEG), axis=0)
    weights = jnp.where(valid_full, jnp.exp(scores - request_peak[safe_owner][..., None]), 0.0)
    member_f = member.astype(jnp.float32)
    totals = jnp.einsum(
        "pr,pkg->rkg", member_f, jnp.sum(weights, axis=-1), precision=lax.Precision.HIGHEST
    )
    page_out = jnp.einsum(
        "pkgt,ptkd->pkgd",
        weights.astype(jnp.bfloat16),
        values_here,
        preferred_element_type=jnp.float32,
    )
    outputs = jnp.einsum("pr,pkgd->rkgd", member_f, page_out, precision=lax.Precision.HIGHEST)
    outputs = outputs.reshape(requests, heads, head_size)
    peaks = request_peak.reshape(requests, heads)
    totals = totals.reshape(requests, heads)
    heads_here = heads // model_count
    parts = (
        outputs.reshape(requests, model_count, heads_here, head_size),
        peaks.reshape(requests, model_count, heads_here),
        totals.reshape(requests, model_count, heads_here),
    )
    blocked = combine_heads(
        (
            lax.all_to_all(parts[0], "mp", split_axis=1, concat_axis=1, tiled=True),
            lax.all_to_all(parts[1], "mp", split_axis=1, concat_axis=1, tiled=True),
            lax.all_to_all(parts[2], "mp", split_axis=1, concat_axis=1, tiled=True),
        )
    )
    merged = combined_all(blocked, "kv", merge_pair)
    attention_output = (
        (merged[0] / merged[2][..., None])
        .astype(jnp.bfloat16)
        .reshape(requests, heads_here * head_size)
    )
    adapter_weights = down_weight_columns.shape[1] // ADAPTER_RANK
    rows_here = requests // model_count
    row_start = lax.axis_index("mp") * rows_here
    select = (
        request_adapter_index[:, None] == jnp.arange(adapter_weights, dtype=jnp.int32)[None, :]
    ).astype(jnp.float32)
    rank_reduced = jnp.dot(
        attention_output, down_weight_columns, preferred_element_type=jnp.float32
    ).reshape(requests, adapter_weights, ADAPTER_RANK)
    rank_part = jnp.sum(rank_reduced * select[:, :, None], axis=1)
    up_weight_float = up_weight_rows.astype(jnp.float32)
    projected_output = lax.psum_scatter(
        jnp.dot(attention_output, output_weight, preferred_element_type=jnp.float32).astype(
            jnp.bfloat16
        ),
        "mp",
        scatter_dimension=0,
        tiled=True,
    ).astype(jnp.float32)
    rank_terms = lax.psum(rank_part, "mp")
    own_rank = lax.dynamic_slice_in_dim(rank_terms, row_start, rows_here, 0)
    own_select = lax.dynamic_slice_in_dim(select, row_start, rows_here, 0)
    expanded_update = (own_select[:, :, None] * own_rank[:, None, :]).reshape(
        own_rank.shape[0], adapter_weights * ADAPTER_RANK
    )
    final_output = projected_output + ADAPTER_SCALE * jnp.dot(
        expanded_update, up_weight_float, precision=lax.Precision.HIGHEST
    )
    return final_output.astype(jnp.bfloat16)


def solution(mesh):
    in_specs = (
        P(None, ("kv", "mp")),
        P("kv", "mp", None, None),
        P(),
        P(),
        P(),
        P("mp", "kv"),
        P("mp", None),
        P(None, "kv"),
    )
    out_specs = P("mp", "kv")
    return jax.shard_map(
        on_device, mesh=mesh, in_specs=in_specs, out_specs=out_specs, check_vma=False
    )
```

profile of v0, /device:TPU:32, one launch (start us, length us, event | category | flops | bytes accessed | tf_op | source)
XLA Modules:
  0.0 474.7 jit_solution(15227640586478832025)
XLA Ops:
  6.5 0.8 broadcast_compare_fusion
  7.3 0.7 broadcast_subtract_fusion
  8.3 4.3 scatter_custom_fusion
  12.8 200.8 %all_gather.21 = bf16[32,8192]{0,1:T(8,128)(2,1)S(1)} all-gather(bf16[32,16]{0,1:T(8,128)(2,1)} %param.10), channel_id=1, replica_groups=mesh['kv'=32,'mp'=16] {'kv','mp'}, dimensions={1}, use_global_device_ids=true | all-gather | bytes 525312 | tf_op jit(solution)/shard_map/all_gather | solution.py:55
  213.7 0.8 copy.100
  214.5 0.7 gather_fusion
  215.2 0.9 gather_fusion.1
  216.2 1.3 fusion.31
  218.5 4.3 scatter_custom_fusion.1
  224.6 0.7 reshape.235
  225.3 3.7 all-to-all-start.2
  229.0 0.9 copy.107
  230.3 0.7 reshape.233
  231.0 5.4 %all-to-all-done.2 = f32[16,1,128]{2,1,0:T(1,128)S(1)} async-done(((f32[16,1,128]{2,1,0:T(1,128)}), f32[16,1,128]{2,1,0:T(1,128)S(1)}, u32[]{:S(2)}, u32[]{:S(2)}) %all-to-all-start.2) | async-done | bytes 8224 | tf_op jit(solution)/shard_map/all_to_all | solution.py:115
  236.4 3.5 all-to-all-start
  239.9 2.3 fusion.7
  242.2 5.1 %all-to-all-done = f32[16,1,128]{2,1,0:T(1,128)S(1)} async-done(((f32[16,1,128]{2,1,0:T(1,128)}), f32[16,1,128]{2,1,0:T(1,128)S(1)}, u32[]{:S(2)}, u32[]{:S(2)}) %all-to-all-start) | async-done | bytes 8224 | tf_op jit(solution)/shard_map/all_to_all | solution.py:114
  247.2 3.7 all-to-all-start.1
  251.6 0.7 reduce.1
  252.4 0.7 reduce
  253.2 13.2 %all-to-all-done.1 = f32[32,16,4,128]{3,0,2,1:T(8,128)S(1)} async-done(((f32[32,16,4,128]{3,0,2,1:T(8,128)}), f32[32,16,4,128]{3,0,2,1:T(8,128)S(1)}, u32[]{:S(2)}, u32[]{:S(2)}) %all-to-all-start.1) | async-done | bytes 1048608 | tf_op jit(solution)/shard_map/all_to_all | solution.py:113
  267.5 1.3 copy.116
  268.8 1.2 dynamic-slice
  270.7 32.4 %all-gather.4 = f32[32,32,4]{1,2,0:T(4,128)S(1)} all-gather(f32[1,32,4]{1,2,0:T(4,128)S(1)} %bitcast.74), channel_id=4, replica_groups=mesh['kv'=32,'mp'=16] {'kv'}, dimensions={0}, use_global_device_ids=true | all-gather | bytes 16896 | tf_op jit(solution)/shard_map/all_gather | solution.py:16
  303.1 30.0 %all-gather.3 = f32[32,32,4]{1,2,0:T(4,128)S(1)} all-gather(f32[1,32,4]{1,2,0:T(4,128)S(1)} %bitcast.73), channel_id=3, replica_groups=mesh['kv'=32,'mp'=16] {'kv'}, dimensions={0}, use_global_device_ids=true | all-gather | bytes 16896 | tf_op jit(solution)/shard_map/all_gather | solution.py:16
  333.1 4.4 all-gather.7.cloned.1.call-done
  337.5 1.7 slice.52
  339.3 13.9 %while.14 = (s32[]{:T(128)}, f32[32,4,128]{2,1,0:T(4,128)S(1)}, f32[32,4]{0,1:T(4,128)S(1)}, f32[32,4]{0,1:T(4,128)S(1)}, f32[31,32,4]{1,2,0:T(4,128)S(1)}, /*in...) while((s32[]{:T(128)}, f32[32,4,128]{2,1,0:T(4,128)S(1)}, f32[32,4]{0,1:T(4,128)S(1)}, ...), condition=%wide.region_9.10_spmd, body=%wide.region_8.9_spmd.sunk | while | flops 49922 | bytes 203869 | solution.py:19
  353.5 2.6 fusion.3
  356.0 40.8 %psum.7 = f32[32,16]{0,1:T(8,128)S(1)} all-reduce(f32[32,16]{0,1:T(8,128)S(1)} %fusion.3), channel_id=1, replica_groups=mesh['kv'=32,'mp'=16] {'mp'}, use_global_device_ids=true, to_apply=%region_12.13 | all-reduce | flops 512 | bytes 4096 | tf_op jit(solution)/shard_map/psum | solution.py:143
  397.4 69.5 %all-reduce = bf16[32,256]{1,0:T(8,128)(2,1)S(1)} all-reduce(bf16[32,256]{1,0:T(8,128)(2,1)S(1)} %convolution_convert_fusion), channel_id=5, replica_groups=mesh['kv'=32,'mp'=16] {'mp'}, use_global_device_ids=true, to_apply=%region_10.11.clone | all-reduce | flops 8192 | bytes 32768
  466.9 0.9 fusion.5
  (185 shorter events, 19.7 us)
Async XLA Ops:
  6.5 460.4 %copy-start = (bf16[1024,256]{1,0:T(8,128)(2,1)S(1)}, bf16[1024,256]{1,0:T(8,128)(2,1)}, u32[]{:S(2)}) copy-start(bf16[1024,256]{1,0:T(8,128)(2,1)} %param.17) | copy-start | bytes 1572868
  12.8 201.6 %copy-start.1 = (s32[32]{0:T(128)S(1)}, s32[32]{0:T(128)}, u32[]{:S(2)}) copy-start(s32[32]{0:T(128)} %param.13) | copy-start | bytes 388
  225.3 11.2 %all-to-all-start.2 = ((f32[16,1,128]{2,1,0:T(1,128)}), f32[16,1,128]{2,1,0:T(1,128)S(1)}, u32[]{:S(2)}, u32[]{:S(2)}) async-start(f32[16,1,128]{2,1,0:T(1,128)} %reshape.235), calls=%async_computation.2 | async-start | bytes 16384 | tf_op jit(solution)/shard_map/all_to_all | solution.py:115
  236.4 10.8 %all-to-all-start = ((f32[16,1,128]{2,1,0:T(1,128)}), f32[16,1,128]{2,1,0:T(1,128)S(1)}, u32[]{:S(2)}, u32[]{:S(2)}) async-start(f32[16,1,128]{2,1,0:T(1,128)} %reshape.233), calls=%async_computation | async-start | bytes 16384 | tf_op jit(solution)/shard_map/all_to_all | solution.py:114
  242.2 25.3 %copy-start.2 = (bf16[512,1024]{1,0:T(8,128)(2,1)S(1)}, bf16[512,1024]{1,0:T(8,128)(2,1)}, u32[]{:S(2)}) copy-start(bf16[512,1024]{1,0:T(8,128)(2,1)} %param.16) | copy-start | bytes 3145732
  247.2 19.2 %all-to-all-start.1 = ((f32[32,16,4,128]{3,0,2,1:T(8,128)}), f32[32,16,4,128]{3,0,2,1:T(8,128)S(1)}, u32[]{:S(2)}, u32[]{:S(2)}) async-start(f32[32,16,4,128]{3,0,2,1:T(8,128)} %bitcast.6), calls=%async_computation.1 | async-start | bytes 2097152 | tf_op jit(solution)/shard_map/all_to_all | solution.py:113
  250.9 19.7 %copy-start.4 = (s32[32]{0:T(128)S(1)}, s32[32]{0:T(128)}, u32[]{:S(2)}) copy-start(s32[32]{0:T(128)} %param.14) | copy-start | bytes 388
  250.9 86.6 %all-gather.7.cloned.1.call-start = ((), (), s32[]{:S(2)}) async-start(), calls=%async_computation.3 | async-start | bytes 2162688 | tf_op jit(solution)/shard_map/all_gather | solution.py:16
  337.5 1.8 slice-start
  339.3 57.9 %copy-start.3 = (bf16[512,256]{1,0:T(8,128)(2,1)S(1)}, bf16[512,256]{1,0:T(8,128)(2,1)}, u32[]{:S(2)}) copy-start(bf16[512,256]{1,0:T(8,128)(2,1)} %param.15) | copy-start | bytes 786436
Sparse Core Ops, SparseCore 0:
  267.6 69.9 all-gather.6
where the time goes:
time: 475 us
  blocking collectives  374 us (79%)
  waiting for transfers between devices  28.1 us (6%)
  local copies, waits for them, and re-layouts  28 us (6%)
  between operations  14.3 us (3%)
  other arithmetic  12.3 us (3%)
  starting transfers between devices  10.9 us (2%)
  matrix products  6.92 us (1%)
    all_gather x1, blocking collectives, on_device(): whole_queries = lax.all_gather(queries, ('kv', 'mp'), axis=1, tiled=True)  201 us
    unnamed x1, blocking collectives  69.5 us
    all_gather x2, blocking collectives, combined_all(): pieces = jax.tree.map(lambda part: lax.all_gather(part, axis), value)  62.4 us
    psum x1, blocking collectives, on_device(): rank_terms = lax.psum(rank_part, 'mp')  40.8 us
    all_to_all x1, waiting for transfers between devices, on_device(): lax.all_to_all(parts[0], 'mp', split_axis=1, concat_axis=1, tiled=True)  13.2 us
  transfers between devices with their start and end apart: 4, of which 4 were waited for; matrix products, arithmetic and copies ran while one was open for 2% of the time, Pallas kernels for 0%

commit v1 on v0

v1 whole, which is shorter than its diff:
```python
import math

import jax
import jax.numpy as jnp
import numpy as np
from jax import lax
from jax.experimental import pallas as pl
from jax.experimental.pallas import tpu as pltpu
from jax.sharding import Mesh
from jax.sharding import PartitionSpec as P

RANK = 16
LOW = -1e30
FLOOR = -1e20
ADAPTER_SCALE = 2.0

KV = ("zh", "zl", "c")
MP = ("y", "xh", "xl")
NEAR = ("zl", "c")
SPLIT = ("zl", "c", "xl")

bf16 = jnp.bfloat16
f32 = jnp.float32


def exchange(value, axes):
    return lax.all_to_all(value, axes, split_axis=0, concat_axis=0, tiled=True)


def call(kernel, out_shape, *operands, scratch=(), vmem=None):
    return pl.pallas_call(
        kernel,
        out_shape=out_shape,
        in_specs=[pl.BlockSpec(memory_space=pltpu.VMEM)] * len(operands),
        out_specs=pl.BlockSpec(memory_space=pltpu.VMEM),
        scratch_shapes=list(scratch),
        compiler_params=pltpu.CompilerParams(vmem_limit_bytes=vmem or 16 * 1024 * 1024),
    )(*operands)


def pack_queries(q_ref, out_ref):
    q = q_ref[...].astype(f32)
    requests, width = q.shape
    lanes = 4 * requests
    row = lax.broadcasted_iota(jnp.int32, (requests, lanes), 0)
    lane = lax.broadcasted_iota(jnp.int32, (requests, lanes), 1)
    packed = jnp.zeros((4, lanes), f32)
    for u in range(4):
        place = (lane == row + u * requests).astype(f32)
        packed = packed + lax.dot_general(
            q[:, 4 * u : 4 * u + 4],
            place,
            (((0,), (0,)), ((), ())),
            preferred_element_type=f32,
        )
    out_ref[...] = jnp.broadcast_to(packed.astype(bf16)[None], out_ref.shape)


def regroup_queries(x_ref, out_ref):
    x = x_ref[...].astype(f32).reshape(8, 4, 4, 128)
    group = lax.broadcasted_iota(jnp.int32, (32, 128), 1) // 32
    blocks = [x[:, i].reshape(32, 128) for i in range(4)]
    rows = []
    for u in range(4):
        merged = jnp.zeros((32, 128), f32)
        for i in range(4):
            moved = pltpu.roll(blocks[i], (32 * (i - u)) % 128, 1) if i != u else blocks[i]
            merged = jnp.where(group == i, moved, merged)
        rows.append(merged.reshape(8, 1, 4, 128))
    whole = jnp.concatenate(rows, axis=1).reshape(8, 16, 128).astype(bf16)
    out_ref[...] = jnp.broadcast_to(whole[:, None], (8, 2, 16, 128)).reshape(16, 16, 128)


def attend(scale, q_ref, kv_ref, count_ref, out_ref, s_ref):
    queries = jnp.concatenate(
        [q_ref[0:8].reshape(128, 128), q_ref[8:16].reshape(128, 128)], axis=1
    )
    parts = kv_ref.shape[0]
    token = lax.broadcasted_iota(jnp.int32, (16, 8, 128), 1)
    room = (count_ref[...][:, None, :] - token).reshape(128, 128)
    room = jnp.concatenate([room, room], axis=1)
    peak = jnp.full((1, 256), FLOOR, f32)
    for j in range(parts):
        scores = jnp.dot(kv_ref[j, :, :128], queries, preferred_element_type=f32) * scale
        scores = jnp.where(room > 8 * j, scores, LOW)
        s_ref[j] = scores
        peak = jnp.maximum(peak, jnp.max(scores, axis=0, keepdims=True))
    total = jnp.zeros((1, 256), f32)
    mixed = jnp.zeros((128, 256), f32)
    for j in range(parts):
        weights = jnp.exp(s_ref[j] - peak)
        total = total + jnp.sum(weights, axis=0, keepdims=True)
        mixed = mixed + lax.dot_general(
            kv_ref[j, :, 128:],
            weights.astype(bf16),
            (((0,), (0,)), ((), ())),
            preferred_element_type=f32,
        )
    outputs = mixed.T
    pair = jnp.concatenate(
        [jnp.broadcast_to(peak, (64, 256)), jnp.broadcast_to(total, (64, 256))], axis=0
    ).T
    for bit0 in range(2):
        for half in range(2):
            for bit1 in range(2):
                for c in range(2):
                    start = ((bit0 * 2 + half) * 2 + bit1) * 32 + 16 * c
                    to = ((bit0 * 2 + bit1) * 2 + c) * 2 + half
                    out_ref[to, 0:16, :] = outputs[start : start + 16]
                    out_ref[to, 16:32, :] = pair[start : start + 16]


def merged(x_ref):
    outputs = x_ref[:, 0:16, :]
    pair = x_ref[:, 16:32, :]
    peaks = pair[:, :, 0:1]
    totals = pair[:, :, 64:65]
    peak = jnp.max(peaks, axis=0)
    factor = jnp.exp(peaks - peak[None])
    total = jnp.sum(factor * totals, axis=0)
    return jnp.sum(factor * outputs, axis=0), peak, total


def merge_near(x_ref, out_ref):
    outputs, peak, total = merged(x_ref)
    lane = lax.broadcasted_iota(jnp.int32, (16, 128), 1)
    pair = jnp.where(lane < 64, peak, total)
    for k in range(out_ref.shape[0]):
        out_ref[k, 0:16, :] = outputs
        out_ref[k, 16:32, :] = pair


def merge_far(x_ref, out_ref):
    outputs, _, total = merged(x_ref)
    attended = (outputs / total).astype(bf16)
    out_ref[...] = jnp.broadcast_to(attended[None], out_ref.shape)


def project(att_ref, adapter_ref, weight_ref, down_ref, up_ref, out_ref):
    att = att_ref[...].reshape(4, 32, 128)
    projected = jnp.zeros((32, 256), f32)
    reduced = jnp.zeros((32, down_ref.shape[1]), f32)
    for part, head in enumerate((0, 2, 1, 3)):
        rows = slice(128 * head, 128 * head + 128)
        projected = projected + jnp.dot(
            att[part], weight_ref[rows, :], preferred_element_type=f32
        )
        reduced = reduced + jnp.dot(att[part], down_ref[rows, :], preferred_element_type=f32)
    column = lax.broadcasted_iota(jnp.int32, reduced.shape, 1)
    chosen = jnp.where(column // RANK == adapter_ref[...], reduced, 0.0)
    upper = chosen.astype(bf16)
    lower = (chosen - upper.astype(f32)).astype(bf16)
    both = jnp.dot(
        jnp.concatenate([upper, lower], axis=0), up_ref[...], preferred_element_type=f32
    )
    result = projected + ADAPTER_SCALE * (both[:32] + both[32:])
    for j in range(16):
        out_ref[j, 0:2, :] = result[2 * j : 2 * j + 2, :128]
        out_ref[j, 2:4, :] = result[2 * j : 2 * j + 2, 128:]


def finish(x_ref, out_ref):
    result = jnp.sum(x_ref[...], axis=0)
    out_ref[:, 0:128] = result[0:2].astype(out_ref.dtype)
    out_ref[:, 128:256] = result[2:4].astype(out_ref.dtype)


def on_device(
    queries,
    key_value_pages,
    request_page_index,
    lengths,
    request_adapter_index,
    output_weight,
    down_weight_columns,
    up_weight_rows,
):
    shape = jax.ShapeDtypeStruct
    requests = lengths.shape[0]
    pages_here, slice_tokens, kv_heads, row = key_value_pages.shape
    page_size = slice_tokens * lax.axis_size(MP)
    scale = 1.0 / math.sqrt(row // 2)

    with jax.named_scope("queries_over_kv"):
        packed = call(pack_queries, shape((32, 4, 128), bf16), queries)
        spread = exchange(packed, KV)
    with jax.named_scope("pages_by_head"):
        half = pages_here // 2
        by_head = key_value_pages.reshape(2, half * slice_tokens, kv_heads, row)
        by_head = by_head.transpose(2, 0, 1, 3).reshape(16, half * slice_tokens, row)
        pages = exchange(by_head, MP)
    with jax.named_scope("counts"):
        first = lax.axis_index(KV) * pages_here + lax.axis_index("xl") * half
        ids = first + jnp.arange(half, dtype=jnp.int32)
        starts = page_size * jnp.arange(request_page_index.shape[1], dtype=jnp.int32)
        inside = jnp.clip(lengths[:, None] - starts[None, :], 0, page_size)
        match = request_page_index[None] == ids[:, None, None]
        count = jnp.sum(jnp.where(match, inside[None], 0), axis=2)
        count = jnp.tile(count, (1, 128 // requests))
    with jax.named_scope("queries_over_mp"):
        regrouped = call(regroup_queries, shape((16, 16, 128), bf16), spread)
        own_queries = exchange(regrouped, MP)
    with jax.named_scope("attention"):
        partial = call(
            lambda *refs: attend(scale, *refs),
            shape((16, 32, 128), f32),
            own_queries,
            pages,
            count,
            scratch=[pltpu.VMEM((16, 128, 256), f32)],
        )
    with jax.named_scope("merge"):
        near = call(merge_near, shape((4, 32, 128), f32), exchange(partial, SPLIT))
        attended = call(merge_far, shape((8, 16, 128), bf16), exchange(near, ("zh",)))
        attended = exchange(attended, NEAR)
    with jax.named_scope("projection"):
        result = call(
            project,
            shape((16, 4, 128), f32),
            attended,
            request_adapter_index[:, None],
            output_weight,
            down_weight_columns,
            up_weight_rows,
        )
        return call(finish, shape((2, 256), bf16), exchange(result, MP))


def solution(mesh):
    fine = Mesh(mesh.devices.reshape(4, 4, 2, 4, 2, 2), KV + MP)
    in_specs = (
        P(None, KV + MP),
        P(KV, MP, None, None),
        P(),
        P(),
        P(),
        P(MP, KV),
        P(MP, None),
        P(None, KV),
    )
    return jax.shard_map(
        on_device, mesh=fine, in_specs=in_specs, out_specs=P(MP, KV), check_vma=False
    )
```

time: 475 us -> 118 us (0.25)
  the two profiles are of different devices: /device:TPU:32 before, /device:TPU:1 now
where the time goes in v1:
time: 118 us
  blocking collectives  70 us (59%)
  waiting for transfers between devices  21.9 us (19%)
  starting transfers between devices  15.4 us (13%)
  Pallas kernels  4.85 us (4%)
  local copies, waits for them, and re-layouts  4.64 us (4%)
    all_to_all x4, blocking collectives, exchange(): return lax.all_to_all(value, axes, split_axis=0, concat_axis=0, tiled=True)  70 us
    all_to_all x3, waiting for transfers between devices, exchange(): return lax.all_to_all(value, axes, split_axis=0, concat_axis=0, tiled=True)  21.9 us
    all_to_all x3, starting transfers between devices, exchange(): return lax.all_to_all(value, axes, split_axis=0, concat_axis=0, tiled=True)  15.4 us
    pallas_call x7, Pallas kernels, call(): pl.pallas_call(kernel, out_shape=out_shape, in_specs=[pl.BlockSpec(memory...  4.85 us
    reshape x1, local copies, waits for them, and re-layouts, on_device(): by_head = key_value_pages.reshape(2, half * slice_tokens, kv_heads, row)  2.42 us
  transfers between devices with their start and end apart: 3, of which 3 were waited for; matrix products, arithmetic and copies ran while one was open for 3% of the time, Pallas kernels for 0%

profile of v1, /device:TPU:1, one launch (start us, length us, event | category | flops | bytes accessed | tf_op | source)
XLA Modules:
  0.0 117.5 jit_solution(4809869987435919586)
XLA Ops:
  0.0 0.8 copy.12.q_ref
  0.8 0.3 queries_over_kv.1
  1.0 28.7 %all_to_all.35.x_ref = bf16[32,4,128]{2,1,0:T(4,128)(2,1)S(1)} all-to-all(bf16[32,4,128]{2,1,0:T(4,128)(2,1)S(1)} %queries_over_kv.1), channel_id=1, replica_groups=mesh['zh'=4,'zl'=4,'c'=2,'y'=4,'xh'=2,'xl'=2] {'zh','zl','c'}, dimensions={0} | all-to-all | bytes 65536 | tf_op jit(solution)/shard_map/queries_over_kv/all_to_all | solution.py:27
  29.7 0.7 queries_over_mp.1
  30.4 6.8 %all-to-all-start.1 = ((bf16[16,16,128]{2,1,0:T(8,128)(2,1)}), bf16[16,16,128]{2,1,0:T(8,128)(2,1)S(1)}, u32[]{:S(2)}, u32[]{:S(2)}) async-start(bf16[16,16,128]{2,1,0:T(8,128)(2,1)} %queries_over_mp.1), calls=%async_computation.1 | async-start | bytes 131072 | tf_op jit(solution)/shard_map/queries_over_mp/all_to_all | solution.py:27
  37.2 2.4 %copy.13 = bf16[2,128,8,256]{3,1,0,2:T(8,128)(2,1)} copy(bf16[2,128,8,256]{3,2,1,0:T(8,128)(2,1)} %bitcast.5) | data formatting | bytes 2097152 | tf_op jit(solution)/shard_map/pages_by_head/reshape | solution.py:189
  39.6 4.1 %all-to-all-done.1.refs_0_ = bf16[16,16,128]{2,1,0:T(8,128)(2,1)S(1)} async-done(((bf16[16,16,128]{2,1,0:T(8,128)(2,1)}), bf16[16,16,128]{2,1,0:T(8,128)(2,1)S(1)}, u32[]{:S(2)}, u32[]{:S(2)}) %all-to-all-start.1) | async-done | bytes 65568 | tf_op jit(solution)/shard_map/queries_over_mp/all_to_all | solution.py:27
  43.7 0.0 copy-start.4
  43.7 3.8 %all-to-all-start.2 = ((bf16[16,128,256]{2,1,0:T(8,128)(2,1)}), bf16[16,128,256]{2,1,0:T(8,128)(2,1)S(1)}, u32[]{:S(2)}, u32[]{:S(2)}) async-start(bf16[16,128,256]{2,1,0:T(8,128)(2,1)} %bitcast.2), calls=%async_computation.2 | async-start | bytes 2097152 | tf_op jit(solution)/shard_map/pages_by_head/all_to_all | solution.py:27
  47.5 0.0 copy-start.3
  47.6 0.0 copy-done.4
  47.6 0.1 subtract_clamp_fusion
  47.6 0.6 copy-done.3
  48.2 0.4 select_reduce_fusion
  48.7 0.1 tile.10.refs_2_
  48.8 13.6 %all-to-all-done.2.refs_1_ = bf16[16,128,256]{2,1,0:T(8,128)(2,1)S(1)} async-done(((bf16[16,128,256]{2,1,0:T(8,128)(2,1)}), bf16[16,128,256]{2,1,0:T(8,128)(2,1)S(1)}, u32[]{:S(2)}, u32[]{:S(2)}) %all-to-all-start.2) | async-done | bytes 1048608 | tf_op jit(solution)/shard_map/pages_by_head/all_to_all | solution.py:27
  62.4 1.8 %attention.1 = f32[16,32,128]{2,1,0:T(8,128)S(1)} custom-call(bf16[16,16,128]{2,1,0:T(8,128)(2,1)S(1)} %all-to-all-done.1.refs_0_, bf16[16,128,256]{2,1,0:T(8,128)(2,1)S(1)} %all-to-all-done.2.refs_1_, s32[16,128]{1,0:T(8,128)S(1)} %tile.10.refs_2_), custom_call_target="tpu_custom_call" | custom-call | tf_op jit(solution)/shard_map/attention/pallas_call | solution.py:31
  64.2 0.0 copy-start.1
  64.2 15.9 %all_to_all.36.x_ref = f32[16,32,128]{2,1,0:T(8,128)S(1)} all-to-all(f32[16,32,128]{2,1,0:T(8,128)S(1)} %attention.1), channel_id=1, replica_groups=mesh['zh'=4,'zl'=4,'c'=2,'y'=4,'xh'=2,'xl'=2] {'zl','c','xl'}, dimensions={0} | all-to-all | bytes 524288 | tf_op jit(solution)/shard_map/merge/all_to_all | solution.py:27
  80.1 0.2 merge.2
  80.2 15.9 %all_to_all.37.x_ref = f32[4,32,128]{2,1,0:T(8,128)S(1)} all-to-all(f32[4,32,128]{2,1,0:T(8,128)S(1)} %merge.2), channel_id=1, replica_groups=mesh['zh'=4,'zl'=4,'c'=2,'y'=4,'xh'=2,'xl'=2] {'zh'}, dimensions={0} | all-to-all | bytes 131072 | tf_op jit(solution)/shard_map/merge/all_to_all | solution.py:27
  96.2 0.8 merge.3
  97.0 4.9 %all-to-all-start.5 = ((bf16[8,16,128]{2,1,0:T(8,128)(2,1)}), bf16[8,16,128]{2,1,0:T(8,128)(2,1)S(1)}, u32[]{:S(2)}, u32[]{:S(2)}) async-start(bf16[8,16,128]{2,1,0:T(8,128)(2,1)} %merge.3), calls=%async_computation.5 | async-start | bytes 65536 | tf_op jit(solution)/shard_map/merge/all_to_all | solution.py:27
  101.8 0.7 copy-done.5
  102.5 0.1 copy.14.adapter_ref
  102.6 4.2 %all-to-all-done.5.att_ref = bf16[8,16,128]{2,1,0:T(8,128)(2,1)S(1)} async-done(((bf16[8,16,128]{2,1,0:T(8,128)(2,1)}), bf16[8,16,128]{2,1,0:T(8,128)(2,1)S(1)}, u32[]{:S(2)}, u32[]{:S(2)}) %all-to-all-start.5) | async-done | bytes 32800 | tf_op jit(solution)/shard_map/merge/all_to_all | solution.py:27
  106.8 0.0 copy-done
  106.8 0.0 copy-done.1
  106.8 0.0 copy-done.2
  106.8 0.5 projection.2
  107.4 9.6 %all_to_all.38.x_ref = f32[16,4,128]{2,1,0:T(4,128)S(1)} all-to-all(f32[16,4,128]{2,1,0:T(4,128)S(1)} %projection.2), channel_id=1, replica_groups=mesh['zh'=4,'zl'=4,'c'=2,'y'=4,'xh'=2,'xl'=2] {'y','xh','xl'}, dimensions={0} | all-to-all | bytes 65536 | tf_op jit(solution)/shard_map/projection/all_to_all | solution.py:27
  116.9 0.6 projection.3
  (6 shorter events, 0.0 us)
Async XLA Ops:
  30.4 13.3 %all-to-all-start.1 = ((bf16[16,16,128]{2,1,0:T(8,128)(2,1)}), bf16[16,16,128]{2,1,0:T(8,128)(2,1)S(1)}, u32[]{:S(2)}, u32[]{:S(2)}) async-start(bf16[16,16,128]{2,1,0:T(8,128)(2,1)} %queries_over_mp.1), calls=%async_computation.1 | async-start | bytes 131072 | tf_op jit(solution)/shard_map/queries_over_mp/all_to_all | solution.py:27
  43.7 3.8 %copy-start.4 = (s32[32]{0:T(128)S(1)}, s32[32]{0:T(128)}, u32[]{:S(2)}) copy-start(s32[32]{0:T(128)} %param.11) | copy-start | bytes 388
  43.7 18.7 %all-to-all-start.2 = ((bf16[16,128,256]{2,1,0:T(8,128)(2,1)}), bf16[16,128,256]{2,1,0:T(8,128)(2,1)S(1)}, u32[]{:S(2)}, u32[]{:S(2)}) async-start(bf16[16,128,256]{2,1,0:T(8,128)(2,1)} %bitcast.2), calls=%async_computation.2 | async-start | bytes 2097152 | tf_op jit(solution)/shard_map/pages_by_head/all_to_all | solution.py:27
  47.5 0.7 copy-start.3
  48.7 58.1 %copy-start = (bf16[512,1024]{1,0:T(8,128)(2,1)S(1)}, bf16[512,1024]{1,0:T(8,128)(2,1)}, u32[]{:S(2)}) copy-start(bf16[512,1024]{1,0:T(8,128)(2,1)} %down_ref.1) | copy-start | bytes 3145732
  64.2 42.6 %copy-start.1 = (bf16[1024,256]{1,0:T(8,128)(2,1)S(1)}, bf16[1024,256]{1,0:T(8,128)(2,1)}, u32[]{:S(2)}) copy-start(bf16[1024,256]{1,0:T(8,128)(2,1)} %up_ref.1) | copy-start | bytes 1572868
  80.1 26.7 %copy-start.2 = (bf16[512,256]{1,0:T(8,128)(2,1)S(1)}, bf16[512,256]{1,0:T(8,128)(2,1)}, u32[]{:S(2)}) copy-start(bf16[512,256]{1,0:T(8,128)(2,1)} %weight_ref.1) | copy-start | bytes 786436
  97.0 9.9 %all-to-all-start.5 = ((bf16[8,16,128]{2,1,0:T(8,128)(2,1)}), bf16[8,16,128]{2,1,0:T(8,128)(2,1)S(1)}, u32[]{:S(2)}, u32[]{:S(2)}) async-start(bf16[8,16,128]{2,1,0:T(8,128)(2,1)} %merge.3), calls=%async_computation.5 | async-start | bytes 65536 | tf_op jit(solution)/shard_map/merge/all_to_all | solution.py:27
  101.8 0.7 copy-start.5

commit v2 on v1

--- a/solution.py
+++ b/solution.py
@@ -14,10 +14,11 @@
 FLOOR = -1e20
 ADAPTER_SCALE = 2.0
 
-KV = ("zh", "zl", "c")
+KV = ("zo", "zn", "c")
 MP = ("y", "xh", "xl")
-NEAR = ("zl", "c")
-SPLIT = ("zl", "c", "xl")
+NEAR = ("zn", "c")
+SPLIT = ("zn", "c", "xl")
+FAR = ("zo",)
 
 bf16 = jnp.bfloat16
 f32 = jnp.float32
@@ -40,19 +41,13 @@
 
 def pack_queries(q_ref, out_ref):
     q = q_ref[...].astype(f32)
-    requests, width = q.shape
-    lanes = 4 * requests
-    row = lax.broadcasted_iota(jnp.int32, (requests, lanes), 0)
-    lane = lax.broadcasted_iota(jnp.int32, (requests, lanes), 1)
-    packed = jnp.zeros((4, lanes), f32)
+    requests = q.shape[1]
+    row = lax.broadcasted_iota(jnp.int32, (requests, 128), 0)
+    lane = lax.broadcasted_iota(jnp.int32, (requests, 128), 1)
+    packed = jnp.zeros((4, 128), f32)
     for u in range(4):
         place = (lane == row + u * requests).astype(f32)
-        packed = packed + lax.dot_general(
-            q[:, 4 * u : 4 * u + 4],
-            place,
-            (((0,), (0,)), ((), ())),
-            preferred_element_type=f32,
-        )
+        packed = packed + jnp.dot(q[4 * u : 4 * u + 4], place, preferred_element_type=f32)
     out_ref[...] = jnp.broadcast_to(packed.astype(bf16)[None], out_ref.shape)
 
 
@@ -71,17 +66,18 @@
     out_ref[...] = jnp.broadcast_to(whole[:, None], (8, 2, 16, 128)).reshape(16, 16, 128)
 
 
-def attend(scale, q_ref, kv_ref, count_ref, out_ref, s_ref):
+def attend(scale, x_ref, count_ref, out_ref, s_ref):
+    queries = x_ref[:, 256:272, :]
     queries = jnp.concatenate(
-        [q_ref[0:8].reshape(128, 128), q_ref[8:16].reshape(128, 128)], axis=1
-    )
-    parts = kv_ref.shape[0]
+        [queries[0:8].reshape(128, 128), queries[8:16].reshape(128, 128)], axis=1
+    )
+    parts = x_ref.shape[0]
     token = lax.broadcasted_iota(jnp.int32, (16, 8, 128), 1)
     room = (count_ref[...][:, None, :] - token).reshape(128, 128)
     room = jnp.concatenate([room, room], axis=1)
     peak = jnp.full((1, 256), FLOOR, f32)
     for j in range(parts):
-        scores = jnp.dot(kv_ref[j, :, :128], queries, preferred_element_type=f32) * scale
+        scores = jnp.dot(x_ref[j, 0:128, :], queries, preferred_element_type=f32) * scale
         scores = jnp.where(room > 8 * j, scores, LOW)
         s_ref[j] = scores
         peak = jnp.maximum(peak, jnp.max(scores, axis=0, keepdims=True))
@@ -91,53 +87,82 @@
         weights = jnp.exp(s_ref[j] - peak)
         total = total + jnp.sum(weights, axis=0, keepdims=True)
         mixed = mixed + lax.dot_general(
-            kv_ref[j, :, 128:],
+            x_ref[j, 128:256, :],
             weights.astype(bf16),
             (((0,), (0,)), ((), ())),
             preferred_element_type=f32,
         )
     outputs = mixed.T
-    pair = jnp.concatenate(
-        [jnp.broadcast_to(peak, (64, 256)), jnp.broadcast_to(total, (64, 256))], axis=0
-    ).T
+    row = lax.broadcasted_iota(jnp.int32, (128, 256), 0)
+    pair = jnp.where(row % 32 < 16, peak, total).T
+    lane = lax.broadcasted_iota(jnp.int32, (8, 128), 1)
     for bit0 in range(2):
         for half in range(2):
             for bit1 in range(2):
-                for c in range(2):
-                    start = ((bit0 * 2 + half) * 2 + bit1) * 32 + 16 * c
-                    to = ((bit0 * 2 + bit1) * 2 + c) * 2 + half
-                    out_ref[to, 0:16, :] = outputs[start : start + 16]
-                    out_ref[to, 16:32, :] = pair[start : start + 16]
-
-
-def merged(x_ref):
-    outputs = x_ref[:, 0:16, :]
-    pair = x_ref[:, 16:32, :]
-    peaks = pair[:, :, 0:1]
-    totals = pair[:, :, 64:65]
+                start = ((bit0 * 2 + half) * 2 + bit1) * 32
+                to = (bit0 * 2 + bit1) * 2 + half
+                out_ref[to, 0:32, :] = outputs[start : start + 32]
+                packed = pair[start : start + 8]
+                for block in range(1, 4):
+                    rows = pair[start + 8 * block : start + 8 * block + 8]
+                    packed = jnp.where(lane // 32 == block, rows, packed)
+                out_ref[to, 32:40, :] = packed
+
+
+def merge(outputs, peaks, totals):
     peak = jnp.max(peaks, axis=0)
     factor = jnp.exp(peaks - peak[None])
-    total = jnp.sum(factor * totals, axis=0)
-    return jnp.sum(factor * outputs, axis=0), peak, total
+    return jnp.sum(factor * outputs, axis=0), peak, jnp.sum(factor * totals, axis=0)
+
+
+def thirds(value):
+    parts = []
+    for _ in range(3):
+        parts.append(value.astype(bf16).astype(f32))
+        value = value - parts[-1]
+    return parts
 
 
 def merge_near(x_ref, out_ref):
-    outputs, peak, total = merged(x_ref)
+    blocks = []
+    for block in range(4):
+        lane = 32 * block
+        blocks.append(
+            merge(
+                x_ref[:, 8 * block : 8 * block + 8, :],
+                x_ref[:, 32:40, lane : lane + 1],
+                x_ref[:, 32:40, lane + 16 : lane + 17],
+            )
+        )
+    outputs, peak, total = (jnp.concatenate(part, axis=0) for part in zip(*blocks))
+    columns = []
+    for rows in (slice(0, 16), slice(16, 32)):
+        columns += thirds(peak[rows]) + thirds(total[rows])
     lane = lax.broadcasted_iota(jnp.int32, (16, 128), 1)
-    pair = jnp.where(lane < 64, peak, total)
-    for k in range(out_ref.shape[0]):
-        out_ref[k, 0:16, :] = outputs
-        out_ref[k, 16:32, :] = pair
+    tile = jnp.zeros((16, 128), f32)
+    for place, column in enumerate(columns):
+        tile = jnp.where(lane // 8 == place, column, tile)
+    whole = jnp.concatenate([outputs, tile], axis=0).astype(bf16)
+    out_ref[...] = jnp.broadcast_to(whole[None], out_ref.shape)
 
 
 def merge_far(x_ref, out_ref):
-    outputs, _, total = merged(x_ref)
-    attended = (outputs / total).astype(bf16)
+    tile = x_ref[:, 32:48, :].astype(f32)
+
+    def column(place):
+        parts = [
+            sum(tile[:, :, 8 * (first + k) : 8 * (first + k) + 1] for k in range(3))
+            for first in (place, place + 6)
+        ]
+        return jnp.concatenate(parts, axis=1)
+
+    outputs, _, total = merge(x_ref[:, 0:32, :].astype(f32), column(0), column(3))
+    attended = (outputs * (1.0 / total)).astype(bf16)
     out_ref[...] = jnp.broadcast_to(attended[None], out_ref.shape)
 
 
 def project(att_ref, adapter_ref, weight_ref, down_ref, up_ref, out_ref):
-    att = att_ref[...].reshape(4, 32, 128)
+    att = att_ref[...]
     projected = jnp.zeros((32, 256), f32)
     reduced = jnp.zeros((32, down_ref.shape[1]), f32)
     for part, head in enumerate((0, 2, 1, 3)):
@@ -181,14 +206,15 @@
     page_size = slice_tokens * lax.axis_size(MP)
     scale = 1.0 / math.sqrt(row // 2)
 
+    half = pages_here // 2
     with jax.named_scope("queries_over_kv"):
-        packed = call(pack_queries, shape((32, 4, 128), bf16), queries)
+        packed = call(pack_queries, shape((32, 4, 128), bf16), queries.T)
         spread = exchange(packed, KV)
     with jax.named_scope("pages_by_head"):
-        half = pages_here // 2
-        by_head = key_value_pages.reshape(2, half * slice_tokens, kv_heads, row)
-        by_head = by_head.transpose(2, 0, 1, 3).reshape(16, half * slice_tokens, row)
-        pages = exchange(by_head, MP)
+        tokens = half * slice_tokens
+        by_head = key_value_pages.reshape(2, tokens, kv_heads, 2, row // 2)
+        by_head = by_head.transpose(2, 0, 3, 1, 4).reshape(16, 2 * tokens, row // 2)
+        by_head = jnp.pad(by_head, ((0, 0), (0, 16), (0, 0)))
     with jax.named_scope("counts"):
         first = lax.axis_index(KV) * pages_here + lax.axis_index("xl") * half
         ids = first + jnp.arange(half, dtype=jnp.int32)
@@ -197,21 +223,22 @@
         match = request_page_index[None] == ids[:, None, None]
         count = jnp.sum(jnp.where(match, inside[None], 0), axis=2)
         count = jnp.tile(count, (1, 128 // requests))
-    with jax.named_scope("queries_over_mp"):
+    with jax.named_scope("queries_and_pages_over_mp"):
+        spread, by_head, count = lax.optimization_barrier((spread, by_head, count))
         regrouped = call(regroup_queries, shape((16, 16, 128), bf16), spread)
-        own_queries = exchange(regrouped, MP)
+        sent = lax.dynamic_update_slice(by_head, regrouped, (0, 2 * tokens, 0))
+        arrived = exchange(sent, MP)
     with jax.named_scope("attention"):
         partial = call(
             lambda *refs: attend(scale, *refs),
-            shape((16, 32, 128), f32),
-            own_queries,
-            pages,
+            shape((8, 40, 128), f32),
+            arrived,
             count,
             scratch=[pltpu.VMEM((16, 128, 256), f32)],
         )
     with jax.named_scope("merge"):
-        near = call(merge_near, shape((4, 32, 128), f32), exchange(partial, SPLIT))
-        attended = call(merge_far, shape((8, 16, 128), bf16), exchange(near, ("zh",)))
+        near = call(merge_near, shape((8, 48, 128), bf16), exchange(partial, SPLIT))
+        attended = call(merge_far, shape((4, 32, 128), bf16), exchange(near, FAR))
         attended = exchange(attended, NEAR)
     with jax.named_scope("projection"):
         result = call(
@@ -227,7 +254,7 @@
 
 
 def solution(mesh):
-    fine = Mesh(mesh.devices.reshape(4, 4, 2, 4, 2, 2), KV + MP)
+    fine = Mesh(mesh.devices.reshape(8, 2, 2, 4, 2, 2), KV + MP)
     in_specs = (
         P(None, KV + MP),
         P(KV, MP, None, None),

time: 118 us -> 102 us (0.86)
  blocking collectives: 70 us -> 58.5 us
  waiting for transfers between devices: 21.9 us -> 11.6 us
  starting transfers between devices: 15.4 us -> 21.8 us
  local copies, waits for them, and re-layouts: 4.64 us -> 2.47 us
  other arithmetic: 0.49 us -> 1.87 us
    all_to_all x4, blocking collectives: 70 us -> 58.5 us  [exchange(): return lax.all_to_all(value, axes, split_axis=0, concat_axis=0, tiled=True)]
    all_to_all x3 -> x2, waiting for transfers between devices: 21.9 us -> 11.6 us  [exchange(): return lax.all_to_all(value, axes, split_axis=0, concat_axis=0, tiled=True)]
    all_to_all x3 -> x2, starting transfers between devices: 15.4 us -> 21.8 us  [exchange(): return lax.all_to_all(value, axes, split_axis=0, concat_axis=0, tiled=True)]
    unnamed x13 -> x10, local copies, waits for them, and re-layouts: 2.04 us -> 0.7 us
  transfers between devices with their start and end apart: 3 -> 2, of which waited for: 3 -> 2; matrix products, arithmetic and copies ran while one was open for 3% -> 4% of each run, Pallas kernels for 0% -> 0%
where the time goes in v2:
time: 102 us; the launch traced here: 101 us
  blocking collectives  58.5 us (57%)
  starting transfers between devices  21.8 us (21%)
  waiting for transfers between devices  11.6 us (11%)
  Pallas kernels  4.92 us (5%)
  local copies, waits for them, and re-layouts  2.47 us (2%)
  other arithmetic  1.87 us (2%)
    all_to_all x4, blocking collectives, exchange(): return lax.all_to_all(value, axes, split_axis=0, concat_axis=0, tiled=True)  58.5 us
    all_to_all x2, starting transfers between devices, exchange(): return lax.all_to_all(value, axes, split_axis=0, concat_axis=0, tiled=True)  21.8 us
    all_to_all x2, waiting for transfers between devices, exchange(): return lax.all_to_all(value, axes, split_axis=0, concat_axis=0, tiled=True)  11.6 us
    pallas_call x7, Pallas kernels, call(): pl.pallas_call(kernel, out_shape=out_shape, in_specs=[pl.BlockSpec(memory...  4.92 us
  transfers between devices with their start and end apart: 2, of which 2 were waited for; matrix products, arithmetic and copies ran while one was open for 4% of the time, Pallas kernels for 0%

profile of v2, /device:TPU:1, one launch (start us, length us, event | category | flops | bytes accessed | tf_op | source)
XLA Modules:
  0.0 101.3 jit_solution(6973666282901401094)
XLA Ops:
  0.0 0.0 copy-start.3
  0.0 0.7 copy-done.3
  0.7 0.7 queries_over_kv.1
  1.4 16.8 %all-to-all-start = ((bf16[32,4,128]{2,1,0:T(4,128)(2,1)}), bf16[32,4,128]{2,1,0:T(4,128)(2,1)S(1)}, u32[]{:S(2)}, u32[]{:S(2)}) async-start(bf16[32,4,128]{2,1,0:T(4,128)(2,1)} %queries_over_kv.1), calls=%async_computation | async-start | bytes 65536 | tf_op jit(solution)/shard_map/queries_over_kv/all_to_all | solution.py:28
  18.2 0.7 subtract_clamp_fusion
  19.0 1.1 %select_reduce_fusion = s32[16,32]{1,0:T(8,128)S(1)} fusion(s32[32,32]{1,0:T(8,128)S(1)} %subtract_clamp_fusion, s32[32,32]{1,0:T(8,128)} %param.10, s32[16]{0:T(128)S(1)} %iota_add_fusion), kind=kLoop, calls=%fused_computation | loop fusion | flops 48640 | bytes 10304 | tf_op jit(solution)/shard_map/counts/reduce_sum | solution.py:224
  20.1 0.1 tile.10.refs_1_
  20.2 1.5 %copy.11 = bf16[2,128,8,2,128]{4,1,3,0,2:T(8,128)(2,1)S(1)} copy(bf16[2,128,8,2,128]{4,2,3,1,0:T(8,128)(2,1)} %bitcast.8) | data formatting | bytes 2097152 | tf_op jit(solution)/shard_map/pages_by_head/reshape | solution.py:215
  21.7 0.1 pad.4
  21.8 8.5 %all-to-all-done.x_ref = bf16[32,4,128]{2,1,0:T(4,128)(2,1)S(1)} async-done(((bf16[32,4,128]{2,1,0:T(4,128)(2,1)}), bf16[32,4,128]{2,1,0:T(4,128)(2,1)S(1)}, u32[]{:S(2)}, u32[]{:S(2)}) %all-to-all-start) | async-done | bytes 32800 | tf_op jit(solution)/shard_map/queries_over_kv/all_to_all | solution.py:28
  30.3 0.1 queries_and_pages_over_mp.1
  30.4 23.3 %all_to_all.30.refs_0_ = bf16[16,272,128]{2,1,0:T(8,128)(2,1)S(1)} all-to-all(bf16[16,272,128]{2,1,0:T(8,128)(2,1)S(1)} %constant_dynamic-update-slice_fusion), channel_id=1, replica_groups=mesh['zo'=8,'zn'=2,'c'=2,'y'=4,'xh'=2,'xl'=2] {'y','xh','xl'}, dimensions={0} | all-to-all | bytes 2228224 | tf_op jit(solution)/shard_map/queries_and_pages_over_mp/all_to_all | solution.py:28
  53.7 0.0 copy-start.4
  53.7 0.0 copy-start
  53.7 0.0 copy-start.1
  53.7 0.0 copy-start.2
  53.7 1.8 %attention.1 = f32[8,40,128]{2,1,0:T(8,128)S(1)} custom-call(bf16[16,272,128]{2,1,0:T(8,128)(2,1)S(1)} %all_to_all.30.refs_0_, s32[16,128]{1,0:T(8,128)S(1)} %tile.10.refs_1_), custom_call_target="tpu_custom_call" | custom-call | tf_op jit(solution)/shard_map/attention/pallas_call | solution.py:32
  55.6 9.4 %all_to_all.31.x_ref = f32[8,40,128]{2,1,0:T(8,128)S(1)} all-to-all(f32[8,40,128]{2,1,0:T(8,128)S(1)} %attention.1), channel_id=1, replica_groups=mesh['zo'=8,'zn'=2,'c'=2,'y'=4,'xh'=2,'xl'=2] {'zn','c','xl'}, dimensions={0} | all-to-all | bytes 327680 | tf_op jit(solution)/shard_map/merge/all_to_all | solution.py:28
  65.0 0.2 merge.2
  65.3 16.3 %all_to_all.32.x_ref = bf16[8,48,128]{2,1,0:T(8,128)(2,1)S(1)} all-to-all(bf16[8,48,128]{2,1,0:T(8,128)(2,1)S(1)} %merge.2), channel_id=1, replica_groups=mesh['zo'=8,'zn'=2,'c'=2,'y'=4,'xh'=2,'xl'=2] {'zo'}, dimensions={0} | all-to-all | bytes 196608 | tf_op jit(solution)/shard_map/merge/all_to_all | solution.py:28
  81.5 0.9 merge.3
  82.5 5.0 %all-to-all-start.4 = ((bf16[4,32,128]{2,1,0:T(8,128)(2,1)}), bf16[4,32,128]{2,1,0:T(8,128)(2,1)S(1)}, u32[]{:S(2)}, u32[]{:S(2)}) async-start(bf16[4,32,128]{2,1,0:T(8,128)(2,1)} %merge.3), calls=%async_computation.4 | async-start | bytes 65536 | tf_op jit(solution)/shard_map/merge/all_to_all | solution.py:28
  87.5 0.0 copy-done.4
  87.5 0.1 copy.12.adapter_ref
  87.6 3.1 %all-to-all-done.4.att_ref = bf16[4,32,128]{2,1,0:T(8,128)(2,1)S(1)} async-done(((bf16[4,32,128]{2,1,0:T(8,128)(2,1)}), bf16[4,32,128]{2,1,0:T(8,128)(2,1)S(1)}, u32[]{:S(2)}, u32[]{:S(2)}) %all-to-all-start.4) | async-done | bytes 32800 | tf_op jit(solution)/shard_map/merge/all_to_all | solution.py:28
  90.7 0.0 copy-done
  90.7 0.0 copy-done.1
  90.7 0.0 copy-done.2
  90.7 0.5 projection.2
  91.2 9.5 %all_to_all.33.x_ref = f32[16,4,128]{2,1,0:T(4,128)S(1)} all-to-all(f32[16,4,128]{2,1,0:T(4,128)S(1)} %projection.2), channel_id=1, replica_groups=mesh['zo'=8,'zn'=2,'c'=2,'y'=4,'xh'=2,'xl'=2] {'y','xh','xl'}, dimensions={0} | all-to-all | bytes 65536 | tf_op jit(solution)/shard_map/projection/all_to_all | solution.py:28
  100.7 0.6 projection.3
  (4 shorter events, 0.0 us)
Async XLA Ops:
  0.0 0.7 copy-start.3
  1.4 28.9 %all-to-all-start = ((bf16[32,4,128]{2,1,0:T(4,128)(2,1)}), bf16[32,4,128]{2,1,0:T(4,128)(2,1)S(1)}, u32[]{:S(2)}, u32[]{:S(2)}) async-start(bf16[32,4,128]{2,1,0:T(4,128)(2,1)} %queries_over_kv.1), calls=%async_computation | async-start | bytes 65536 | tf_op jit(solution)/shard_map/queries_over_kv/all_to_all | solution.py:28
  53.7 33.7 %copy-start.4 = (s32[32]{0:T(128)S(1)}, s32[32]{0:T(128)}, u32[]{:S(2)}) copy-start(s32[32]{0:T(128)} %param.12) | copy-start | bytes 388
  53.7 36.9 %copy-start = (bf16[512,1024]{1,0:T(8,128)(2,1)S(1)}, bf16[512,1024]{1,0:T(8,128)(2,1)}, u32[]{:S(2)}) copy-start(bf16[512,1024]{1,0:T(8,128)(2,1)} %down_ref.1) | copy-start | bytes 3145732
  53.7 36.9 %copy-start.1 = (bf16[1024,256]{1,0:T(8,128)(2,1)S(1)}, bf16[1024,256]{1,0:T(8,128)(2,1)}, u32[]{:S(2)}) copy-start(bf16[1024,256]{1,0:T(8,128)(2,1)} %up_ref.1) | copy-start | bytes 1572868
  53.7 36.9 %copy-start.2 = (bf16[512,256]{1,0:T(8,128)(2,1)S(1)}, bf16[512,256]{1,0:T(8,128)(2,1)}, u32[]{:S(2)}) copy-start(bf16[512,256]{1,0:T(8,128)(2,1)} %weight_ref.1) | copy-start | bytes 786436
  82.5 8.2 %all-to-all-start.4 = ((bf16[4,32,128]{2,1,0:T(8,128)(2,1)}), bf16[4,32,128]{2,1,0:T(8,128)(2,1)S(1)}, u32[]{:S(2)}, u32[]{:S(2)}) async-start(bf16[4,32,128]{2,1,0:T(8,128)(2,1)} %merge.3), calls=%async_computation.4 | async-start | bytes 65536 | tf_op jit(solution)/shard_map/merge/all_to_all | solution.py:28

commit v3 on v2

v3 whole, which is shorter than its diff:
```python
import math

import jax
import jax.numpy as jnp
from jax import lax
from jax.experimental import pallas as pl
from jax.experimental.pallas import tpu as pltpu
from jax.sharding import Mesh
from jax.sharding import PartitionSpec as P

RANK = 16
LOW = -1e30
FLOOR = -1e20
ADAPTER_SCALE = 2.0

KV = ("zo", "zn", "c")
MP = ("y", "x")
NEAR = ("zn", "c")
SPLIT = ("zn", "c", "x")
FAR = ("zo",)

bf16 = jnp.bfloat16
f32 = jnp.float32
i32 = jnp.int32


QUERY_FIRST = 24
MERGE_FIRST = 3


def exchange(value, axes, first=0):
    members = value.shape[0]
    groups = [[(first + k) % members for k in range(members)]] if first else None
    return lax.all_to_all(
        value, axes, split_axis=0, concat_axis=0, tiled=True, axis_index_groups=groups
    )


def call(kernel, out_shape, *operands, scratch=(), cost=None):
    return pl.pallas_call(
        kernel,
        out_shape=out_shape,
        in_specs=[pl.BlockSpec(memory_space=pltpu.VMEM)] * len(operands),
        out_specs=jax.tree.map(lambda _: pl.BlockSpec(memory_space=pltpu.VMEM), out_shape),
        scratch_shapes=list(scratch),
        cost_estimate=cost,
        compiler_params=pltpu.CompilerParams(vmem_limit_bytes=16 * 1024 * 1024),
    )(*operands)


def prepare(page_size, *refs):
    given, outs, held, scratch = refs[0:5], refs[5:12], refs[12:16], refs[16:]
    out_ref, count_ref, own_ref, *piece_refs = outs
    kv_ref, wide_ref, packed_ref, sems = scratch
    loads = [
        pltpu.make_async_copy(from_ref, to_ref, sems.at[k])
        for k, (from_ref, to_ref) in enumerate(zip(given, held))
    ]
    parts = 4
    pages = kv_ref.shape[0] // parts
    kv_loads = [
        pltpu.make_async_copy(
            given[4].at[pl.ds(pages * k, pages)], kv_ref.at[pl.ds(pages * k, pages)], sems.at[4 + k]
        )
        for k in range(parts)
    ]
    for load in loads + kv_loads:
        load.start()
    q_ref, table_ref, length_ref, adapter_ref = held
    loads[0].wait()
    q = q_ref[...].astype(f32)
    requests = q.shape[1]
    row = lax.broadcasted_iota(i32, (requests, 128), 0)
    lane = lax.broadcasted_iota(i32, (requests, 128), 1)
    packed = jnp.zeros((4, 128), f32)
    for u in range(4):
        place = (lane == row + u * requests).astype(f32)
        packed = packed + jnp.dot(q[4 * u : 4 * u + 4], place, preferred_element_type=f32)
    packed_ref[...] = jnp.broadcast_to(packed.astype(bf16)[None], packed_ref.shape)
    store = pltpu.make_async_copy(packed_ref, out_ref, sems.at[8])
    store.start()
    tokens = pages * kv_ref.shape[1]
    y = lax.axis_index("y")
    for k, load in enumerate(kv_loads):
        load.wait()
        wide = kv_ref[pages * k : pages * k + pages].astype(f32).reshape(8 * tokens, 256)
        wide_ref[0] = wide[:, :128]
        wide_ref[1] = wide[:, 128:]
        for step, piece_ref in enumerate(piece_refs):
            for head in range(2):
                first = 2 * lax.rem(y + step, 4) + head
                for side in range(2):
                    rows = wide_ref[side, pl.ds(first, tokens, stride=8), :]
                    to = slice(tokens * k, tokens * k + tokens)
                    piece_ref[head, side, to, :] = rows.astype(bf16)
    for load in loads[1:]:
        load.wait()
    pages = count_ref.shape[0]
    first = lax.axis_index(KV) * pages
    table = jnp.concatenate([table_ref[...]] * 4, axis=0).astype(f32)
    table = jnp.concatenate([table] * 4, axis=1).T[: table_ref.shape[1]].astype(i32)
    length = jnp.concatenate([length_ref[...]] * 4, axis=1)
    start = page_size * lax.broadcasted_iota(i32, table.shape, 0)
    inside = jnp.clip(length - start, 0, page_size).astype(f32)
    for page in range(pages):
        found = jnp.where(table == first + page, inside, 0.0)
        count_ref[page : page + 1, :] = jnp.sum(found, axis=0, keepdims=True)
    adapter = jnp.concatenate([adapter_ref[...]] * 4, axis=1).astype(f32)
    adapter = jnp.sum(jnp.where(lane == row, adapter, 0.0), axis=1, keepdims=True)
    own_ref[...] = jnp.broadcast_to(adapter, own_ref.shape).astype(i32)
    store.wait()


def regroup_queries(x_ref, out_ref):
    x = x_ref[...].astype(f32)
    x = jnp.concatenate([x[32 - QUERY_FIRST :], x[: 32 - QUERY_FIRST]], axis=0)
    x = x.reshape(8, 4, 4, 128)
    group = lax.broadcasted_iota(i32, (32, 128), 1) // 32
    blocks = [x[:, i].reshape(32, 128) for i in range(4)]
    rows = []
    for u in range(4):
        merged = jnp.zeros((32, 128), f32)
        for i in range(4):
            moved = pltpu.roll(blocks[i], (32 * (i - u)) % 128, 1) if i != u else blocks[i]
            merged = jnp.where(group == i, moved, merged)
        rows.append(merged.reshape(8, 1, 4, 128))
    whole = jnp.concatenate(rows, axis=1).reshape(4, 1, 2, 16, 128).astype(bf16)
    out_ref[...] = jnp.broadcast_to(whole, (4, 4, 2, 16, 128)).reshape(16, 2, 16, 128)


def thirds(value):
    parts = []
    for _ in range(3):
        parts.append(value.astype(bf16).astype(f32))
        value = value - parts[-1]
    return parts


def encode(outputs, peak, total):
    columns = []
    for rows in (slice(0, 16), slice(16, 32)):
        columns += thirds(peak[rows]) + thirds(total[rows])
    lane = lax.broadcasted_iota(i32, (16, 128), 1)
    tile = jnp.zeros((16, 128), f32)
    for place, column in enumerate(columns):
        tile = jnp.where(lane // 8 == place, column, tile)
    return jnp.concatenate([outputs, tile], axis=0).astype(bf16)


def merged(x_ref):
    tile = x_ref[:, 32:48, :].astype(f32)

    def column(place):
        parts = [
            sum(tile[:, :, 8 * (first + k) : 8 * (first + k) + 1] for k in range(3))
            for first in (place, place + 6)
        ]
        return jnp.concatenate(parts, axis=1)

    peaks, totals = column(0), column(3)
    peak = jnp.max(peaks, axis=0)
    factor = jnp.exp(peaks - peak[None])
    outputs = jnp.sum(factor * x_ref[:, 0:32, :].astype(f32), axis=0)
    return outputs, peak, jnp.sum(factor * totals, axis=0)


def merge_near(x_ref, out_ref):
    out_ref[...] = jnp.broadcast_to(encode(*merged(x_ref))[None], out_ref.shape)


def merge_far(x_ref, out_ref):
    outputs, _, total = merged(x_ref)
    attended = (outputs * (1.0 / total)).astype(bf16)
    out_ref[...] = jnp.broadcast_to(attended[None], out_ref.shape)


def attend(scale, q_ref, own_ref, *refs):
    *piece_refs, count_ref, out_ref, s_ref = refs
    y, x = lax.axis_index("y"), lax.axis_index("x")
    pages = count_ref.shape[0]
    tokens = 8 * pages
    token = lax.broadcasted_iota(i32, (pages, 8, 128), 1)
    room = (count_ref[...].astype(i32)[:, None, :] - token).reshape(tokens, 128)
    room = jnp.concatenate([room, room], axis=1)
    pieces = [own_ref] + list(piece_refs)
    places = [8 * (4 * lax.rem(y + 4 - step, 4) + x) for step in range(4)]
    for head in range(2):
        queries = q_ref[:, head]
        queries = jnp.concatenate(
            [queries[0:8].reshape(128, 128), queries[8:16].reshape(128, 128)], axis=1
        )
        peak = jnp.full((1, 256), FLOOR, f32)
        for step in range(4):
            scores = jnp.dot(pieces[step][head, 0], queries, preferred_element_type=f32)
            scores = jnp.where(room > places[step], scores * scale, LOW)
            s_ref[step] = scores
            peak = jnp.maximum(peak, jnp.max(scores, axis=0, keepdims=True))
        total = jnp.zeros((1, 256), f32)
        mixed = jnp.zeros((128, 256), f32)
        for step in range(4):
            weights = jnp.exp(s_ref[step] - peak)
            total = total + jnp.sum(weights, axis=0, keepdims=True)
            mixed = mixed + lax.dot_general(
                pieces[step][head, 1],
                weights.astype(bf16),
                (((0,), (0,)), ((), ())),
                preferred_element_type=f32,
            )
        outputs = mixed.T
        row = lax.broadcasted_iota(i32, (128, 256), 0)
        pair = jnp.where(row < 64, peak, total).T
        for bit0 in range(2):
            for half in range(2):
                for bit1 in range(2):
                    start = ((bit0 * 2 + half) * 2 + bit1) * 32
                    rows = slice(start, start + 32)
                    to = (bit0 * 2 + bit1) * 4 + head * 2 + half
                    out_ref[to] = encode(outputs[rows], pair[rows, 0:1], pair[rows, 64:65])


def project(att_ref, adapter_ref, weight_ref, down_ref, up_ref, out_ref, rows_ref):
    projected = jnp.zeros((32, 256), f32)
    reduced = jnp.zeros((32, down_ref.shape[1]), f32)
    for part, head in enumerate((0, 2, 1, 3)):
        rows = slice(128 * head, 128 * head + 128)
        projected = projected + jnp.dot(
            att_ref[part], weight_ref[rows, :], preferred_element_type=f32
        )
        reduced = reduced + jnp.dot(att_ref[part], down_ref[rows, :], preferred_element_type=f32)
    column = lax.broadcasted_iota(i32, reduced.shape, 1)
    chosen = jnp.where(column // RANK == adapter_ref[:, 0:1], reduced, 0.0)
    upper = chosen.astype(bf16)
    lower = (chosen - upper.astype(f32)).astype(bf16)
    both = jnp.dot(
        jnp.concatenate([upper, lower], axis=0), up_ref[...], preferred_element_type=f32
    )
    result = projected + ADAPTER_SCALE * (both[:32] + both[32:])
    for j in range(16):
        rows_ref[j, 0:2, :] = result[2 * j : 2 * j + 2, :128]
        rows_ref[j, 2:4, :] = result[2 * j : 2 * j + 2, 128:]
    out_ref[...] = rows_ref[...].astype(bf16)


def finish(x_ref, out_ref):
    result = jnp.sum(x_ref[...].astype(f32), axis=0)
    out_ref[:, 0:128] = result[0:2].astype(out_ref.dtype)
    out_ref[:, 128:256] = result[2:4].astype(out_ref.dtype)


def on_device(
    queries,
    key_value_pages,
    request_page_index,
    lengths,
    request_adapter_index,
    output_weight,
    down_weight_columns,
    up_weight_rows,
):
    shape = jax.ShapeDtypeStruct
    pages_here, slice_tokens, kv_heads, row = key_value_pages.shape
    page_size = slice_tokens * lax.axis_size(MP)
    scale = 1.0 / math.sqrt(row // 2)

    with jax.named_scope("queries_over_kv"):
        tokens = pages_here * slice_tokens
        given = (
            queries.T,
            request_page_index,
            lengths[None],
            request_adapter_index[None],
            key_value_pages,
        )
        anywhere = pl.BlockSpec(memory_space=pl.ANY)
        local = pl.BlockSpec(memory_space=pltpu.VMEM)
        packed, count, adapter, own, *pieces = pl.pallas_call(
            lambda *refs: prepare(page_size, *refs),
            out_shape=(
                shape((32, 4, 128), bf16),
                shape((pages_here, 128), f32),
                shape((32, 128), i32),
            )
            + (shape((2, 2, tokens, row // 2), bf16),) * 4,
            in_specs=[anywhere] * 5,
            out_specs=(anywhere,) + (local,) * 6,
            scratch_shapes=[pltpu.VMEM(part.shape, part.dtype) for part in given]
            + [
                pltpu.VMEM((2, tokens // 4 * kv_heads, row // 2), f32),
                pltpu.VMEM((32, 4, 128), bf16),
                pltpu.SemaphoreType.DMA((9,)),
            ],
        )(*given)
        spread = exchange(packed, KV, QUERY_FIRST)
    with jax.named_scope("pages_over_y"):
        for step in range(1, 4):
            ring = [(k, (k + step) % 4) for k in range(4)]
            pieces[step - 1] = lax.ppermute(pieces[step - 1], "y", ring)
    with jax.named_scope("queries_over_mp"):
        regrouped = call(
            regroup_queries,
            shape((16, 2, 16, 128), bf16),
            spread,
            cost=pl.CostEstimate(flops=10**11, bytes_accessed=10**8, transcendentals=0),
        )
        own_queries = exchange(regrouped, MP)
    with jax.named_scope("attention"):
        partial = call(
            lambda *refs: attend(scale, *refs),
            shape((16, 48, 128), bf16),
            own_queries,
            own,
            *pieces,
            count,
            scratch=[pltpu.VMEM((4, 256, 256), f32)],
        )
    with jax.named_scope("merge"):
        near = call(merge_near, shape((8, 48, 128), bf16), exchange(partial, SPLIT))
        attended = call(merge_far, shape((4, 32, 128), bf16), exchange(near, FAR, MERGE_FIRST))
        attended = exchange(attended, NEAR)
    with jax.named_scope("projection"):
        result = call(
            project,
            shape((16, 4, 128), bf16),
            attended,
            adapter,
            output_weight,
            down_weight_columns,
            up_weight_rows,
            scratch=[pltpu.VMEM((16, 4, 128), f32)],
        )
        return call(finish, shape((2, 256), bf16), exchange(result, MP))


def solution(mesh):
    fine = Mesh(mesh.devices.reshape(8, 2, 2, 4, 4), KV + MP)
    in_specs = (
        P(None, KV + MP),
        P(KV, MP, None, None),
        P(),
        P(),
        P(),
        P(MP, KV),
        P(MP, None),
        P(None, KV),
    )
    return jax.shard_map(
        on_device, mesh=fine, in_specs=in_specs, out_specs=P(MP, KV), check_vma=False
    )
```

time: 102 us -> 91.5 us (0.90)
  waiting for transfers between devices: 11.6 us -> 0.01 us
  starting transfers between devices: 21.8 us -> 27.7 us
  local copies, waits for them, and re-layouts: 2.47 us -> 0.03 us
  other arithmetic: 1.87 us -> 0 us
  blocking collectives: 58.5 us -> 56.9 us
  Pallas kernels: 4.92 us -> 6.25 us
    all_to_all x2 -> x1, waiting for transfers between devices: 11.6 us -> 0.01 us  [exchange(): lax.all_to_all(value, axes, split_axis=0, concat_axis=0, tiled=True, axis...]
    ppermute x0 -> x3, starting transfers between devices: none -> 10.7 us  [on_device(): pieces[step - 1] = lax.ppermute(pieces[step - 1], 'y', ring)]
    all_to_all x2 -> x1, starting transfers between devices: 21.8 us -> 17 us  [exchange(): lax.all_to_all(value, axes, split_axis=0, concat_axis=0, tiled=True, axis...]
    pallas_call x0 -> x1, Pallas kernels: none -> 2.81 us  [on_device(): pl.pallas_call(lambda *refs: prepare(page_size, *refs), out_shape=(shape(...]
    all_to_all x4 -> x5, blocking collectives: 58.5 us -> 56.9 us  [exchange(): lax.all_to_all(value, axes, split_axis=0, concat_axis=0, tiled=True, axis...]
    reshape x1 -> x0, local copies, waits for them, and re-layouts: 1.5 us -> none  [on_device(): by_head = key_value_pages.reshape(2, tokens, kv_heads, 2, row // 2)]
    pallas_call x7 -> x6, Pallas kernels: 4.92 us -> 3.44 us  [call(): pl.pallas_call(kernel, out_shape=out_shape, in_specs=[pl.BlockSpec(memory...]
    reduce_sum x1 -> x0, other arithmetic: 1.13 us -> none  [on_device(): count = jnp.sum(jnp.where(match, inside[None], 0), axis=2)]
  transfers between devices with their start and end apart: 2 -> 4, of which waited for: 2 -> 0; matrix products, arithmetic and copies ran while one was open for 4% -> 0% of each run, Pallas kernels for 0% -> 0%
where the time goes in v3:
time: 91.5 us; the launch traced here: 91 us
  blocking collectives  56.9 us (62%)
  starting transfers between devices  27.7 us (30%)
  Pallas kernels  6.25 us (7%)
    all_to_all x5, blocking collectives, exchange(): lax.all_to_all(value, axes, split_axis=0, concat_axis=0, tiled=True, axis...  56.9 us
    all_to_all x1, starting transfers between devices, exchange(): lax.all_to_all(value, axes, split_axis=0, concat_axis=0, tiled=True, axis...  17 us
    ppermute x3, starting transfers between devices, on_device(): pieces[step - 1] = lax.ppermute(pieces[step - 1], 'y', ring)  10.7 us
    pallas_call x6, Pallas kernels, call(): pl.pallas_call(kernel, out_shape=out_shape, in_specs=[pl.BlockSpec(memory...  3.44 us
    pallas_call x1, Pallas kernels, on_device(): pl.pallas_call(lambda *refs: prepare(page_size, *refs), out_shape=(shape(...  2.81 us
  transfers between devices with their start and end apart: 4, of which 0 were waited for; matrix products, arithmetic and copies ran while one was open for 0% of the time, Pallas kernels for 0%

profile of v3, /device:TPU:1, one launch (start us, length us, event | category | flops | bytes accessed | tf_op | source)
XLA Modules:
  0.0 91.0 jit_solution(13880880168291818067)
XLA Ops:
  0.0 2.8 %queries_over_kv.1 = (bf16[32,4,128]{2,1,0:T(4,128)(2,1)}, f32[32,128]{1,0:T(8,128)}, s32[32,128]{1,0:T(8,128)}, bf16[2,2,256,128]{3,2,1,0:T(8,128)(2,1)}, bf16[...) custom-call(bf16[16,32]{1,0:T(8,128)(2,1)} %bitcast.3, ...), custom_call_target="tpu_custom_call" | custom-call | tf_op jit(solution)/shard_map/queries_over_kv/pallas_call | solution.py:276
  2.8 17.0 %all-to-all-start = ((bf16[32,4,128]{2,1,0:T(4,128)(2,1)}), bf16[32,4,128]{2,1,0:T(4,128)(2,1)S(1)}, u32[]{:S(2)}, u32[]{:S(2)}) async-start(bf16[32,4,128]{2,1,0:T(4,128)(2,1)} %get-tuple-element.12), calls=%async_computation | async-start | bytes 65536 | tf_op jit(solution)/shard_map/queries_over_kv/all_to_all | solution.py:34
  19.8 3.2 %collective-permute-start = (bf16[2,2,256,128]{3,2,1,0:T(8,128)(2,1)}, bf16[2,2,256,128]{3,2,1,0:T(8,128)(2,1)S(1)}, u32[]{:S(2)}, u32[]{:S(2)}) collective-permute-start(bf16[2,2,256,128]{3,2,1,0:T(8,128)(2,1)} %get-tuple-element.14), channel_id=1, source_target_pairs={{0,4},{4,8},{8,12},{12,0},{1,5},{5,9},{9,13},{13,1},{2,6},{6,10},{... | collective-permute-start | bytes 786440 | tf_op jit(solution)/shard_map/pages_over_y/ppermute | solution.py:297
  23.0 4.5 %collective-permute-start.1 = (bf16[2,2,256,128]{3,2,1,0:T(8,128)(2,1)}, bf16[2,2,256,128]{3,2,1,0:T(8,128)(2,1)S(1)}, u32[]{:S(2)}, u32[]{:S(2)}) collective-permute-start(bf16[2,2,256,128]{3,2,1,0:T(8,128)(2,1)} %get-tuple-element.15), channel_id=1, source_target_pairs={{0,8},{4,12},{8,0},{12,4},{1,9},{5,13},{9,1},{13,5},{2,10},{6,14},... | collective-permute-start | bytes 786440 | tf_op jit(solution)/shard_map/pages_over_y/ppermute | solution.py:297
  27.5 3.0 %collective-permute-start.2 = (bf16[2,2,256,128]{3,2,1,0:T(8,128)(2,1)}, bf16[2,2,256,128]{3,2,1,0:T(8,128)(2,1)S(1)}, u32[]{:S(2)}, u32[]{:S(2)}) collective-permute-start(bf16[2,2,256,128]{3,2,1,0:T(8,128)(2,1)} %get-tuple-element.16), channel_id=1, source_target_pairs={{0,12},{4,0},{8,4},{12,8},{1,13},{5,1},{9,5},{13,9},{2,14},{6,2},{... | collective-permute-start | bytes 786440 | tf_op jit(solution)/shard_map/pages_over_y/ppermute | solution.py:297
  30.5 0.0 all-to-all-done.x_ref
  30.5 0.0 copy-start.4
  30.5 0.1 queries_over_mp.1
  30.7 0.0 copy-start.2
  30.7 11.0 %all_to_all.30.refs_0_ = bf16[16,2,16,128]{3,2,1,0:T(8,128)(2,1)S(1)} all-to-all(bf16[16,2,16,128]{3,2,1,0:T(8,128)(2,1)S(1)} %queries_over_mp.1), channel_id=1, replica_groups=mesh['zo'=8,'zn'=2,'c'=2,'y'=4,'x'=4] {'y','x'}, dimensions={0} | all-to-all | bytes 262144 | tf_op jit(solution)/shard_map/queries_over_mp/all_to_all | solution.py:34
  41.7 0.0 collective-permute-done.refs_2_
  41.7 0.0 collective-permute-done.1.refs_3_
  41.7 0.0 collective-permute-done.2.refs_4_
  41.7 0.0 copy-done.4
  41.7 0.0 copy-done.2
  41.7 0.0 copy-start
  41.7 1.5 %attention.1 = bf16[16,48,128]{2,1,0:T(8,128)(2,1)S(1)} custom-call(bf16[16,2,16,128]{3,2,1,0:T(8,128)(2,1)S(1)} %all_to_all.30.refs_0_, bf16[2,2,256,128]{3,2,1,0:T(8,128)(2,1)S(1)} %copy-done.2, bf16[2,2,256,128]{3,2,1,0:T(8,128)(2,1)S(1)} %collective-permute-done.refs_2_, bf16[2,2,256,128]{3,2,1,0:T(8,128)(2,1)S(1)} %collective-permute-done.1.refs_3_, ...), custom_call_target="tpu_custom_call" | custom-call | tf_op jit(solution)/shard_map/attention/pallas_call | solution.py:40
  43.2 0.0 copy-start.1
  43.2 12.8 %all_to_all.31.x_ref = bf16[16,48,128]{2,1,0:T(8,128)(2,1)S(1)} all-to-all(bf16[16,48,128]{2,1,0:T(8,128)(2,1)S(1)} %attention.1), channel_id=1, replica_groups=mesh['zo'=8,'zn'=2,'c'=2,'y'=4,'x'=4] {'zn','c','x'}, dimensions={0} | all-to-all | bytes 393216 | tf_op jit(solution)/shard_map/merge/all_to_all | solution.py:34
  56.0 0.4 merge.2
  56.5 0.0 copy-start.3
  56.5 16.0 %all_to_all.32.x_ref = bf16[8,48,128]{2,1,0:T(8,128)(2,1)S(1)} all-to-all(bf16[8,48,128]{2,1,0:T(8,128)(2,1)S(1)} %merge.2), channel_id=1, replica_groups={{192,256,320,384,448,0,64,128},{193,257,321,385,449,1,65,129},{194,258,..., dimensions={0} | all-to-all | bytes 196608 | tf_op jit(solution)/shard_map/merge/all_to_all | solution.py:34
  72.5 0.3 merge.3
  72.8 0.0 copy-start.5
  72.8 7.3 %all_to_all.33.att_ref = bf16[4,32,128]{2,1,0:T(8,128)(2,1)S(1)} all-to-all(bf16[4,32,128]{2,1,0:T(8,128)(2,1)S(1)} %merge.3), channel_id=1, replica_groups=mesh['zo'=8,'zn'=2,'c'=2,'y'=4,'x'=4] {'zn','c'}, dimensions={0} | all-to-all | bytes 65536 | tf_op jit(solution)/shard_map/merge/all_to_all | solution.py:34
  80.1 0.0 copy-done
  80.1 0.0 copy-done.1
  80.1 0.0 copy-done.3
  80.1 0.0 copy-done.5
  80.1 0.5 projection.2
  80.6 9.8 %all_to_all.34.x_ref = bf16[16,4,128]{2,1,0:T(4,128)(2,1)S(1)} all-to-all(bf16[16,4,128]{2,1,0:T(4,128)(2,1)S(1)} %projection.2), channel_id=1, replica_groups=mesh['zo'=8,'zn'=2,'c'=2,'y'=4,'x'=4] {'y','x'}, dimensions={0} | all-to-all | bytes 32768 | tf_op jit(solution)/shard_map/projection/all_to_all | solution.py:34
  90.4 0.6 projection.3
Async XLA Ops:
  2.8 27.7 %all-to-all-start = ((bf16[32,4,128]{2,1,0:T(4,128)(2,1)}), bf16[32,4,128]{2,1,0:T(4,128)(2,1)S(1)}, u32[]{:S(2)}, u32[]{:S(2)}) async-start(bf16[32,4,128]{2,1,0:T(4,128)(2,1)} %get-tuple-element.12), calls=%async_computation | async-start | bytes 65536 | tf_op jit(solution)/shard_map/queries_over_kv/all_to_all | solution.py:34
  19.8 21.9 %collective-permute-start = (bf16[2,2,256,128]{3,2,1,0:T(8,128)(2,1)}, bf16[2,2,256,128]{3,2,1,0:T(8,128)(2,1)S(1)}, u32[]{:S(2)}, u32[]{:S(2)}) collective-permute-start(bf16[2,2,256,128]{3,2,1,0:T(8,128)(2,1)} %get-tuple-element.14), channel_id=1, source_target_pairs={{0,4},{4,8},{8,12},{12,0},{1,5},{5,9},{9,13},{13,1},{2,6},{6,10},{... | collective-permute-start | bytes 786440 | tf_op jit(solution)/shard_map/pages_over_y/ppermute | solution.py:297
  23.0 18.7 %collective-permute-start.1 = (bf16[2,2,256,128]{3,2,1,0:T(8,128)(2,1)}, bf16[2,2,256,128]{3,2,1,0:T(8,128)(2,1)S(1)}, u32[]{:S(2)}, u32[]{:S(2)}) collective-permute-start(bf16[2,2,256,128]{3,2,1,0:T(8,128)(2,1)} %get-tuple-element.15), channel_id=1, source_target_pairs={{0,8},{4,12},{8,0},{12,4},{1,9},{5,13},{9,1},{13,5},{2,10},{6,14},... | collective-permute-start | bytes 786440 | tf_op jit(solution)/shard_map/pages_over_y/ppermute | solution.py:297
  27.5 14.1 %collective-permute-start.2 = (bf16[2,2,256,128]{3,2,1,0:T(8,128)(2,1)}, bf16[2,2,256,128]{3,2,1,0:T(8,128)(2,1)S(1)}, u32[]{:S(2)}, u32[]{:S(2)}) collective-permute-start(bf16[2,2,256,128]{3,2,1,0:T(8,128)(2,1)} %get-tuple-element.16), channel_id=1, source_target_pairs={{0,12},{4,0},{8,4},{12,8},{1,13},{5,1},{9,5},{13,9},{2,14},{6,2},{... | collective-permute-start | bytes 786440 | tf_op jit(solution)/shard_map/pages_over_y/ppermute | solution.py:297
  30.5 11.2 %copy-start.4 = (f32[32,128]{1,0:T(8,128)S(1)}, f32[32,128]{1,0:T(8,128)}, u32[]{:S(2)}) copy-start(f32[32,128]{1,0:T(8,128)} %get-tuple-element.17.refs_5_) | copy-start | bytes 49156
  30.7 11.0 %copy-start.2 = (bf16[2,2,256,128]{3,2,1,0:T(8,128)(2,1)S(1)}, bf16[2,2,256,128]{3,2,1,0:T(8,128)(2,1)}, u32[]{:S(2)}) copy-start(bf16[2,2,256,128]{3,2,1,0:T(8,128)(2,1)} %get-tuple-element.13.refs_1_) | copy-start | bytes 786436
  41.7 38.4 %copy-start = (bf16[512,1024]{1,0:T(8,128)(2,1)S(1)}, bf16[512,1024]{1,0:T(8,128)(2,1)}, u32[]{:S(2)}) copy-start(bf16[512,1024]{1,0:T(8,128)(2,1)} %down_ref.1) | copy-start | bytes 3145732
  43.2 36.9 %copy-start.1 = (bf16[1024,256]{1,0:T(8,128)(2,1)S(1)}, bf16[1024,256]{1,0:T(8,128)(2,1)}, u32[]{:S(2)}) copy-start(bf16[1024,256]{1,0:T(8,128)(2,1)} %up_ref.1) | copy-start | bytes 1572868
  56.5 23.6 %copy-start.3 = (bf16[512,256]{1,0:T(8,128)(2,1)S(1)}, bf16[512,256]{1,0:T(8,128)(2,1)}, u32[]{:S(2)}) copy-start(bf16[512,256]{1,0:T(8,128)(2,1)} %weight_ref.1) | copy-start | bytes 786436
  72.8 7.3 %copy-start.5 = (s32[32,128]{1,0:T(8,128)S(1)}, s32[32,128]{1,0:T(8,128)}, u32[]{:S(2)}) copy-start(s32[32,128]{1,0:T(8,128)} %get-tuple-element.18.adapter_ref) | copy-start | bytes 49156

commit v4 on v3

--- a/solution.py
+++ b/solution.py
@@ -48,26 +48,7 @@
     )(*operands)
 
 
-def prepare(page_size, *refs):
-    given, outs, held, scratch = refs[0:5], refs[5:12], refs[12:16], refs[16:]
-    out_ref, count_ref, own_ref, *piece_refs = outs
-    kv_ref, wide_ref, packed_ref, sems = scratch
-    loads = [
-        pltpu.make_async_copy(from_ref, to_ref, sems.at[k])
-        for k, (from_ref, to_ref) in enumerate(zip(given, held))
-    ]
-    parts = 4
-    pages = kv_ref.shape[0] // parts
-    kv_loads = [
-        pltpu.make_async_copy(
-            given[4].at[pl.ds(pages * k, pages)], kv_ref.at[pl.ds(pages * k, pages)], sems.at[4 + k]
-        )
-        for k in range(parts)
-    ]
-    for load in loads + kv_loads:
-        load.start()
-    q_ref, table_ref, length_ref, adapter_ref = held
-    loads[0].wait()
+def pack_queries(q_ref, out_ref):
     q = q_ref[...].astype(f32)
     requests = q.shape[1]
     row = lax.broadcasted_iota(i32, (requests, 128), 0)
@@ -76,13 +57,16 @@
     for u in range(4):
         place = (lane == row + u * requests).astype(f32)
         packed = packed + jnp.dot(q[4 * u : 4 * u + 4], place, preferred_element_type=f32)
-    packed_ref[...] = jnp.broadcast_to(packed.astype(bf16)[None], packed_ref.shape)
-    store = pltpu.make_async_copy(packed_ref, out_ref, sems.at[8])
-    store.start()
+    out_ref[...] = jnp.broadcast_to(packed.astype(bf16)[None], out_ref.shape)
+
+
+def sort_pages(kv_ref, *refs):
+    *piece_refs, wide_ref = refs
+    parts = 4
+    pages = kv_ref.shape[0] // parts
     tokens = pages * kv_ref.shape[1]
     y = lax.axis_index("y")
-    for k, load in enumerate(kv_loads):
-        load.wait()
+    for k in range(parts):
         wide = kv_ref[pages * k : pages * k + pages].astype(f32).reshape(8 * tokens, 256)
         wide_ref[0] = wide[:, :128]
         wide_ref[1] = wide[:, 128:]
@@ -93,22 +77,20 @@
                     rows = wide_ref[side, pl.ds(first, tokens, stride=8), :]
                     to = slice(tokens * k, tokens * k + tokens)
                     piece_ref[head, side, to, :] = rows.astype(bf16)
-    for load in loads[1:]:
-        load.wait()
-    pages = count_ref.shape[0]
+
+
+def count_tokens(page_size, pages, table_ref, length_ref):
     first = lax.axis_index(KV) * pages
     table = jnp.concatenate([table_ref[...]] * 4, axis=0).astype(f32)
     table = jnp.concatenate([table] * 4, axis=1).T[: table_ref.shape[1]].astype(i32)
-    length = jnp.concatenate([length_ref[...]] * 4, axis=1)
+    length = jnp.concatenate([length_ref[...].reshape(1, 32)] * 4, axis=1)
     start = page_size * lax.broadcasted_iota(i32, table.shape, 0)
     inside = jnp.clip(length - start, 0, page_size).astype(f32)
-    for page in range(pages):
-        found = jnp.where(table == first + page, inside, 0.0)
-        count_ref[page : page + 1, :] = jnp.sum(found, axis=0, keepdims=True)
-    adapter = jnp.concatenate([adapter_ref[...]] * 4, axis=1).astype(f32)
-    adapter = jnp.sum(jnp.where(lane == row, adapter, 0.0), axis=1, keepdims=True)
-    own_ref[...] = jnp.broadcast_to(adapter, own_ref.shape).astype(i32)
-    store.wait()
+    rows = [
+        jnp.sum(jnp.where(table == first + page, inside, 0.0), axis=0, keepdims=True)
+        for page in range(pages)
+    ]
+    return jnp.concatenate(rows, axis=0).astype(i32)
 
 
 def regroup_queries(x_ref, out_ref):
@@ -138,29 +120,31 @@
 
 def encode(outputs, peak, total):
     columns = []
-    for rows in (slice(0, 16), slice(16, 32)):
+    for block in range(4):
+        rows = slice(8 * block, 8 * block + 8)
         columns += thirds(peak[rows]) + thirds(total[rows])
-    lane = lax.broadcasted_iota(i32, (16, 128), 1)
-    tile = jnp.zeros((16, 128), f32)
+    lane = lax.broadcasted_iota(i32, (8, 128), 1)
+    tile = jnp.zeros((8, 128), f32)
     for place, column in enumerate(columns):
-        tile = jnp.where(lane // 8 == place, column, tile)
+        tile = jnp.where(lane // 5 == place, column, tile)
     return jnp.concatenate([outputs, tile], axis=0).astype(bf16)
 
 
 def merged(x_ref):
-    tile = x_ref[:, 32:48, :].astype(f32)
+    x = x_ref[...].astype(f32)
+    tile = x[:, 32:40]
 
     def column(place):
         parts = [
-            sum(tile[:, :, 8 * (first + k) : 8 * (first + k) + 1] for k in range(3))
-            for first in (place, place + 6)
+            sum(tile[:, :, 5 * (first + k) : 5 * (first + k) + 1] for k in range(3))
+            for first in range(place, 24, 6)
         ]
         return jnp.concatenate(parts, axis=1)
 
     peaks, totals = column(0), column(3)
     peak = jnp.max(peaks, axis=0)
     factor = jnp.exp(peaks - peak[None])
-    outputs = jnp.sum(factor * x_ref[:, 0:32, :].astype(f32), axis=0)
+    outputs = jnp.sum(factor * x[:, 0:32], axis=0)
     return outputs, peak, jnp.sum(factor * totals, axis=0)
 
 
@@ -174,15 +158,15 @@
     out_ref[...] = jnp.broadcast_to(attended[None], out_ref.shape)
 
 
-def attend(scale, q_ref, own_ref, *refs):
-    *piece_refs, count_ref, out_ref, s_ref = refs
+def attend(scale, page_size, q_ref, *refs):
+    *pieces, table_ref, length_ref, adapter_ref, out_ref, own_ref, s_ref = refs
     y, x = lax.axis_index("y"), lax.axis_index("x")
-    pages = count_ref.shape[0]
-    tokens = 8 * pages
+    tokens = pieces[0].shape[2]
+    pages = tokens // 8
+    count = count_tokens(page_size, pages, table_ref, length_ref)
     token = lax.broadcasted_iota(i32, (pages, 8, 128), 1)
-    room = (count_ref[...].astype(i32)[:, None, :] - token).reshape(tokens, 128)
+    room = (count[:, None, :] - token).reshape(tokens, 128)
     room = jnp.concatenate([room, room], axis=1)
-    pieces = [own_ref] + list(piece_refs)
     places = [8 * (4 * lax.rem(y + 4 - step, 4) + x) for step in range(4)]
     for head in range(2):
         queries = q_ref[:, head]
@@ -216,6 +200,11 @@
                     rows = slice(start, start + 32)
                     to = (bit0 * 2 + bit1) * 4 + head * 2 + half
                     out_ref[to] = encode(outputs[rows], pair[rows, 0:1], pair[rows, 64:65])
+    row = lax.broadcasted_iota(i32, own_ref.shape, 0)
+    lane = lax.broadcasted_iota(i32, own_ref.shape, 1)
+    adapter = jnp.concatenate([adapter_ref[...].reshape(1, 32)] * 4, axis=1).astype(f32)
+    adapter = jnp.sum(jnp.where(lane == row, adapter, 0.0), axis=1, keepdims=True)
+    own_ref[...] = jnp.broadcast_to(adapter, own_ref.shape).astype(i32)
 
 
 def project(att_ref, adapter_ref, weight_ref, down_ref, up_ref, out_ref, rows_ref):
@@ -263,38 +252,25 @@
     scale = 1.0 / math.sqrt(row // 2)
 
     with jax.named_scope("queries_over_kv"):
-        tokens = pages_here * slice_tokens
-        given = (
+        packed = call(
+            pack_queries,
+            shape((32, 4, 128), bf16),
             queries.T,
-            request_page_index,
-            lengths[None],
-            request_adapter_index[None],
-            key_value_pages,
-        )
-        anywhere = pl.BlockSpec(memory_space=pl.ANY)
-        local = pl.BlockSpec(memory_space=pltpu.VMEM)
-        packed, count, adapter, own, *pieces = pl.pallas_call(
-            lambda *refs: prepare(page_size, *refs),
-            out_shape=(
-                shape((32, 4, 128), bf16),
-                shape((pages_here, 128), f32),
-                shape((32, 128), i32),
-            )
-            + (shape((2, 2, tokens, row // 2), bf16),) * 4,
-            in_specs=[anywhere] * 5,
-            out_specs=(anywhere,) + (local,) * 6,
-            scratch_shapes=[pltpu.VMEM(part.shape, part.dtype) for part in given]
-            + [
-                pltpu.VMEM((2, tokens // 4 * kv_heads, row // 2), f32),
-                pltpu.VMEM((32, 4, 128), bf16),
-                pltpu.SemaphoreType.DMA((9,)),
-            ],
-        )(*given)
+            cost=pl.CostEstimate(flops=10**10, bytes_accessed=10**7, transcendentals=0),
+        )
         spread = exchange(packed, KV, QUERY_FIRST)
     with jax.named_scope("pages_over_y"):
+        tokens = pages_here * slice_tokens
+        pieces = call(
+            sort_pages,
+            (shape((2, 2, tokens, row // 2), bf16),) * 4,
+            key_value_pages,
+            scratch=[pltpu.VMEM((2, tokens // 4 * kv_heads, row // 2), f32)],
+        )
+        pieces = list(pieces)
         for step in range(1, 4):
             ring = [(k, (k + step) % 4) for k in range(4)]
-            pieces[step - 1] = lax.ppermute(pieces[step - 1], "y", ring)
+            pieces[step] = lax.ppermute(pieces[step], "y", ring)
     with jax.named_scope("queries_over_mp"):
         regrouped = call(
             regroup_queries,
@@ -304,17 +280,18 @@
         )
         own_queries = exchange(regrouped, MP)
     with jax.named_scope("attention"):
-        partial = call(
-            lambda *refs: attend(scale, *refs),
-            shape((16, 48, 128), bf16),
+        partial, adapter = call(
+            lambda *refs: attend(scale, page_size, *refs),
+            (shape((16, 40, 128), bf16), shape((32, 128), i32)),
             own_queries,
-            own,
             *pieces,
-            count,
+            request_page_index,
+            lengths,
+            request_adapter_index,
             scratch=[pltpu.VMEM((4, 256, 256), f32)],
         )
     with jax.named_scope("merge"):
-        near = call(merge_near, shape((8, 48, 128), bf16), exchange(partial, SPLIT))
+        near = call(merge_near, shape((8, 40, 128), bf16), exchange(partial, SPLIT))
         attended = call(merge_far, shape((4, 32, 128), bf16), exchange(near, FAR, MERGE_FIRST))
         attended = exchange(attended, NEAR)
     with jax.named_scope("projection"):

time: 91.5 us -> 89.9 us (0.983)
  Pallas kernels: 6.25 us -> 4.8 us
  blocking collectives: 56.9 us -> 55.5 us
  local copies, waits for them, and re-layouts: 0.03 us -> 1.35 us
    pallas_call x1 -> x0, Pallas kernels: 2.81 us -> none  [on_device(): pl.pallas_call(lambda *refs: prepare(page_size, *refs), out_shape=(shape(...]
    all_to_all x5, blocking collectives: 56.9 us -> 55.5 us  [exchange(): lax.all_to_all(value, axes, split_axis=0, concat_axis=0, tiled=True, axis...]
    pallas_call x6 -> x8, Pallas kernels: 3.44 us -> 4.8 us  [call(): pl.pallas_call(kernel, out_shape=out_shape, in_specs=[pl.BlockSpec(memory...]
    unnamed x12 -> x16, local copies, waits for them, and re-layouts: 0.03 us -> 1.35 us
  transfers between devices with their start and end apart: 4 -> 4, of which waited for: 0 -> 0; matrix products, arithmetic and copies ran while one was open for 0% -> 0% of each run, Pallas kernels for 0% -> 1%
where the time goes in v4:
time: 89.9 us; the launch traced here: 89.4 us
  blocking collectives  55.5 us (62%)
  starting transfers between devices  27.7 us (31%)
  Pallas kernels  4.8 us (5%)
  local copies, waits for them, and re-layouts  1.35 us (2%)
    all_to_all x5, blocking collectives, exchange(): lax.all_to_all(value, axes, split_axis=0, concat_axis=0, tiled=True, axis...  55.5 us
    all_to_all x1, starting transfers between devices, exchange(): lax.all_to_all(value, axes, split_axis=0, concat_axis=0, tiled=True, axis...  17 us
    ppermute x3, starting transfers between devices, on_device(): pieces[step] = lax.ppermute(pieces[step], 'y', ring)  10.7 us
    pallas_call x8, Pallas kernels, call(): pl.pallas_call(kernel, out_shape=out_shape, in_specs=[pl.BlockSpec(memory...  4.8 us
  transfers between devices with their start and end apart: 4, of which 0 were waited for; matrix products, arithmetic and copies ran while one was open for 0% of the time, Pallas kernels for 1%

profile of v4, /device:TPU:1, one launch (start us, length us, event | category | flops | bytes accessed | tf_op | source)
XLA Modules:
  0.0 89.4 jit_solution(1143169136901733898)
XLA Ops:
  0.0 0.0 copy-start.7
  0.0 0.7 copy-done.7
  0.7 0.0 copy-start
  0.7 0.7 queries_over_kv.1
  1.4 17.0 %all-to-all-start = ((bf16[32,4,128]{2,1,0:T(4,128)(2,1)}), bf16[32,4,128]{2,1,0:T(4,128)(2,1)S(1)}, u32[]{:S(2)}, u32[]{:S(2)}) async-start(bf16[32,4,128]{2,1,0:T(4,128)(2,1)} %queries_over_kv.1), calls=%async_computation | async-start | bytes 65536 | tf_op jit(solution)/shard_map/queries_over_kv/all_to_all | solution.py:34
  18.4 0.0 copy-done
  18.4 0.5 pages_over_y.1
  18.9 3.2 %collective-permute-start = (bf16[2,2,256,128]{3,2,1,0:T(8,128)(2,1)S(1)}, bf16[2,2,256,128]{3,2,1,0:T(8,128)(2,1)S(1)}, u32[]{:S(2)}, u32[]{:S(2)}) collective-permute-start(bf16[2,2,256,128]{3,2,1,0:T(8,128)(2,1)S(1)} %get-tuple-element.12), channel_id=1, source_target_pairs={{0,4},{4,8},{8,12},{12,0},{1,5},{5,9},{9,13},{13,1},{2,6},{6,10},{... | collective-permute-start | bytes 786440 | tf_op jit(solution)/shard_map/pages_over_y/ppermute | solution.py:273
  22.2 4.5 %collective-permute-start.1 = (bf16[2,2,256,128]{3,2,1,0:T(8,128)(2,1)S(1)}, bf16[2,2,256,128]{3,2,1,0:T(8,128)(2,1)S(1)}, u32[]{:S(2)}, u32[]{:S(2)}) collective-permute-start(bf16[2,2,256,128]{3,2,1,0:T(8,128)(2,1)S(1)} %get-tuple-element.13), channel_id=1, source_target_pairs={{0,8},{4,12},{8,0},{12,4},{1,9},{5,13},{9,1},{13,5},{2,10},{6,14},... | collective-permute-start | bytes 786440 | tf_op jit(solution)/shard_map/pages_over_y/ppermute | solution.py:273
  26.7 3.0 %collective-permute-start.2 = (bf16[2,2,256,128]{3,2,1,0:T(8,128)(2,1)S(1)}, bf16[2,2,256,128]{3,2,1,0:T(8,128)(2,1)S(1)}, u32[]{:S(2)}, u32[]{:S(2)}) collective-permute-start(bf16[2,2,256,128]{3,2,1,0:T(8,128)(2,1)S(1)} %get-tuple-element.14), channel_id=1, source_target_pairs={{0,12},{4,0},{8,4},{12,8},{1,13},{5,1},{9,5},{13,9},{2,14},{6,2},{... | collective-permute-start | bytes 786440 | tf_op jit(solution)/shard_map/pages_over_y/ppermute | solution.py:273
  29.7 0.0 all-to-all-done.x_ref
  29.7 0.1 queries_over_mp.1
  29.8 0.0 copy-start.4
  29.8 10.9 %all_to_all.30.refs_0_ = bf16[16,2,16,128]{3,2,1,0:T(8,128)(2,1)S(1)} all-to-all(bf16[16,2,16,128]{3,2,1,0:T(8,128)(2,1)S(1)} %queries_over_mp.1), channel_id=1, replica_groups=mesh['zo'=8,'zn'=2,'c'=2,'y'=4,'x'=4] {'y','x'}, dimensions={0} | all-to-all | bytes 262144 | tf_op jit(solution)/shard_map/queries_over_mp/all_to_all | solution.py:34
  40.7 0.0 collective-permute-done.refs_2_
  40.7 0.0 collective-permute-done.1.refs_3_
  40.7 0.0 collective-permute-done.2.refs_4_
  40.7 0.0 copy-done.4
  40.7 0.6 copy-done.5
  41.4 0.0 copy-done.6
  41.4 1.5 %attention.1 = (bf16[16,40,128]{2,1,0:T(8,128)(2,1)S(1)}, s32[32,128]{1,0:T(8,128)S(1)}) custom-call(bf16[16,2,16,128]{3,2,1,0:T(8,128)(2,1)S(1)} %all_to_all.30.refs_0_, bf16[2,2,256,128]{3,2,1,0:T(8,128)(2,1)S(1)} %get-tuple-element.11.refs_1_, bf16[2,2,256,128]{3,2,1,0:T(8,128)(2,1)S(1)} %collective-permute-done.refs_2_, ...), custom_call_target="tpu_custom_call" | custom-call | tf_op jit(solution)/shard_map/attention/pallas_call | solution.py:40
  42.9 12.5 %all_to_all.31.x_ref = bf16[16,40,128]{2,1,0:T(8,128)(2,1)S(1)} all-to-all(bf16[16,40,128]{2,1,0:T(8,128)(2,1)S(1)} %get-tuple-element.15), channel_id=1, replica_groups=mesh['zo'=8,'zn'=2,'c'=2,'y'=4,'x'=4] {'zn','c','x'}, dimensions={0} | all-to-all | bytes 327680 | tf_op jit(solution)/shard_map/merge/all_to_all | solution.py:34
  55.3 0.5 merge.2
  55.8 14.8 %all_to_all.32.x_ref = bf16[8,40,128]{2,1,0:T(8,128)(2,1)S(1)} all-to-all(bf16[8,40,128]{2,1,0:T(8,128)(2,1)S(1)} %merge.2), channel_id=1, replica_groups={{192,256,320,384,448,0,64,128},{193,257,321,385,449,1,65,129},{194,258,..., dimensions={0} | all-to-all | bytes 163840 | tf_op jit(solution)/shard_map/merge/all_to_all | solution.py:34
  70.6 0.3 merge.3
  70.9 7.7 %all_to_all.33.att_ref = bf16[4,32,128]{2,1,0:T(8,128)(2,1)S(1)} all-to-all(bf16[4,32,128]{2,1,0:T(8,128)(2,1)S(1)} %merge.3), channel_id=1, replica_groups=mesh['zo'=8,'zn'=2,'c'=2,'y'=4,'x'=4] {'zn','c'}, dimensions={0} | all-to-all | bytes 65536 | tf_op jit(solution)/shard_map/merge/all_to_all | solution.py:34
  78.6 0.0 copy-done.1
  78.6 0.0 copy-done.2
  78.6 0.0 copy-done.3
  78.6 0.5 projection.2
  79.2 9.7 %all_to_all.34.x_ref = bf16[16,4,128]{2,1,0:T(4,128)(2,1)S(1)} all-to-all(bf16[16,4,128]{2,1,0:T(4,128)(2,1)S(1)} %projection.2), channel_id=1, replica_groups=mesh['zo'=8,'zn'=2,'c'=2,'y'=4,'x'=4] {'y','x'}, dimensions={0} | all-to-all | bytes 32768 | tf_op jit(solution)/shard_map/projection/all_to_all | solution.py:34
  88.8 0.6 projection.3
  (5 shorter events, 0.0 us)
Async XLA Ops:
  0.0 0.7 copy-start.7
  0.7 17.7 %copy-start = (bf16[32,8,8,256]{3,2,1,0:T(8,128)(2,1)S(1)}, bf16[32,8,8,256]{3,2,1,0:T(8,128)(2,1)}, u32[]{:S(2)}) copy-start(bf16[32,8,8,256]{3,2,1,0:T(8,128)(2,1)} %kv_ref.1) | copy-start | bytes 3145732
  1.4 28.2 %all-to-all-start = ((bf16[32,4,128]{2,1,0:T(4,128)(2,1)}), bf16[32,4,128]{2,1,0:T(4,128)(2,1)S(1)}, u32[]{:S(2)}, u32[]{:S(2)}) async-start(bf16[32,4,128]{2,1,0:T(4,128)(2,1)} %queries_over_kv.1), calls=%async_computation | async-start | bytes 65536 | tf_op jit(solution)/shard_map/queries_over_kv/all_to_all | solution.py:34
  18.9 21.8 %collective-permute-start = (bf16[2,2,256,128]{3,2,1,0:T(8,128)(2,1)S(1)}, bf16[2,2,256,128]{3,2,1,0:T(8,128)(2,1)S(1)}, u32[]{:S(2)}, u32[]{:S(2)}) collective-permute-start(bf16[2,2,256,128]{3,2,1,0:T(8,128)(2,1)S(1)} %get-tuple-element.12), channel_id=1, source_target_pairs={{0,4},{4,8},{8,12},{12,0},{1,5},{5,9},{9,13},{13,1},{2,6},{6,10},{... | collective-permute-start | bytes 786440 | tf_op jit(solution)/shard_map/pages_over_y/ppermute | solution.py:273
  22.2 18.5 %collective-permute-start.1 = (bf16[2,2,256,128]{3,2,1,0:T(8,128)(2,1)S(1)}, bf16[2,2,256,128]{3,2,1,0:T(8,128)(2,1)S(1)}, u32[]{:S(2)}, u32[]{:S(2)}) collective-permute-start(bf16[2,2,256,128]{3,2,1,0:T(8,128)(2,1)S(1)} %get-tuple-element.13), channel_id=1, source_target_pairs={{0,8},{4,12},{8,0},{12,4},{1,9},{5,13},{9,1},{13,5},{2,10},{6,14},... | collective-permute-start | bytes 786440 | tf_op jit(solution)/shard_map/pages_over_y/ppermute | solution.py:273
  26.7 14.0 %collective-permute-start.2 = (bf16[2,2,256,128]{3,2,1,0:T(8,128)(2,1)S(1)}, bf16[2,2,256,128]{3,2,1,0:T(8,128)(2,1)S(1)}, u32[]{:S(2)}, u32[]{:S(2)}) collective-permute-start(bf16[2,2,256,128]{3,2,1,0:T(8,128)(2,1)S(1)} %get-tuple-element.14), channel_id=1, source_target_pairs={{0,12},{4,0},{8,4},{12,8},{1,13},{5,1},{9,5},{13,9},{2,14},{6,2},{... | collective-permute-start | bytes 786440 | tf_op jit(solution)/shard_map/pages_over_y/ppermute | solution.py:273
  29.8 10.9 %copy-start.4 = (s32[32,32]{1,0:T(8,128)S(1)}, s32[32,32]{1,0:T(8,128)}, u32[]{:S(2)}) copy-start(s32[32,32]{1,0:T(8,128)} %refs_5_.1) | copy-start | bytes 12292
  40.7 0.7 copy-start.5
  40.7 0.7 copy-start.6
  41.4 37.2 %copy-start.1 = (bf16[512,1024]{1,0:T(8,128)(2,1)S(1)}, bf16[512,1024]{1,0:T(8,128)(2,1)}, u32[]{:S(2)}) copy-start(bf16[512,1024]{1,0:T(8,128)(2,1)} %down_ref.1) | copy-start | bytes 3145732
  42.9 35.7 %copy-start.2 = (bf16[1024,256]{1,0:T(8,128)(2,1)S(1)}, bf16[1024,256]{1,0:T(8,128)(2,1)}, u32[]{:S(2)}) copy-start(bf16[1024,256]{1,0:T(8,128)(2,1)} %up_ref.1) | copy-start | bytes 1572868
  55.3 23.3 %copy-start.3 = (bf16[512,256]{1,0:T(8,128)(2,1)S(1)}, bf16[512,256]{1,0:T(8,128)(2,1)}, u32[]{:S(2)}) copy-start(bf16[512,256]{1,0:T(8,128)(2,1)} %weight_ref.1) | copy-start | bytes 786436

commit v5 on v4

--- a/solution.py
+++ b/solution.py
@@ -154,8 +154,7 @@
 
 def merge_far(x_ref, out_ref):
     outputs, _, total = merged(x_ref)
-    attended = (outputs * (1.0 / total)).astype(bf16)
-    out_ref[...] = jnp.broadcast_to(attended[None], out_ref.shape)
+    out_ref[...] = (outputs * (1.0 / total)).astype(bf16)
 
 
 def attend(scale, page_size, q_ref, *refs):
@@ -292,8 +291,8 @@
         )
     with jax.named_scope("merge"):
         near = call(merge_near, shape((8, 40, 128), bf16), exchange(partial, SPLIT))
-        attended = call(merge_far, shape((4, 32, 128), bf16), exchange(near, FAR, MERGE_FIRST))
-        attended = exchange(attended, NEAR)
+        attended = call(merge_far, shape((32, 128), bf16), exchange(near, FAR, MERGE_FIRST))
+        attended = lax.all_gather(attended, NEAR)
     with jax.named_scope("projection"):
         result = call(
             project,

time: 89.9 us -> 88.2 us (0.981)
  blocking collectives: 55.5 us -> 54.4 us
    all_to_all x5 -> x4, blocking collectives: 55.5 us -> 47.7 us  [exchange(): lax.all_to_all(value, axes, split_axis=0, concat_axis=0, tiled=True, axis...]
    all_gather x0 -> x1, blocking collectives: none -> 6.67 us  [on_device(): attended = lax.all_gather(attended, NEAR)]
where the time goes in v5:
time: 88.2 us; the launch traced here: 87.7 us
  blocking collectives  54.4 us (62%)
  starting transfers between devices  27.7 us (31%)
  Pallas kernels  4.8 us (5%)
    all_to_all x4, blocking collectives, exchange(): lax.all_to_all(value, axes, split_axis=0, concat_axis=0, tiled=True, axis...  47.7 us
    all_to_all x1, starting transfers between devices, exchange(): lax.all_to_all(value, axes, split_axis=0, concat_axis=0, tiled=True, axis...  17 us
    ppermute x3, starting transfers between devices, on_device(): pieces[step] = lax.ppermute(pieces[step], 'y', ring)  10.7 us
    all_gather x1, blocking collectives, on_device(): attended = lax.all_gather(attended, NEAR)  6.67 us
    pallas_call x8, Pallas kernels, call(): pl.pallas_call(kernel, out_shape=out_shape, in_specs=[pl.BlockSpec(memory...  4.8 us
  transfers between devices with their start and end apart: 4, of which 0 were waited for; matrix products, arithmetic and copies ran while one was open for 0% of the time, Pallas kernels for 1%

profile of v5, /device:TPU:1, one launch (start us, length us, event | category | flops | bytes accessed | tf_op | source)
XLA Modules:
  0.0 87.7 jit_solution(6884342125314792176)
XLA Ops:
  0.0 0.7 copy-done.7
  0.7 0.7 queries_over_kv.1
  1.4 17.0 %all-to-all-start = ((bf16[32,4,128]{2,1,0:T(4,128)(2,1)}), bf16[32,4,128]{2,1,0:T(4,128)(2,1)S(1)}, u32[]{:S(2)}, u32[]{:S(2)}) async-start(bf16[32,4,128]{2,1,0:T(4,128)(2,1)} %queries_over_kv.1), calls=%async_computation | async-start | bytes 65536 | tf_op jit(solution)/shard_map/queries_over_kv/all_to_all | solution.py:34
  18.4 0.0 copy-done
  18.4 0.5 pages_over_y.1
  18.9 3.2 %collective-permute-start = (bf16[2,2,256,128]{3,2,1,0:T(8,128)(2,1)S(1)}, bf16[2,2,256,128]{3,2,1,0:T(8,128)(2,1)S(1)}, u32[]{:S(2)}, u32[]{:S(2)}) collective-permute-start(bf16[2,2,256,128]{3,2,1,0:T(8,128)(2,1)S(1)} %get-tuple-element.12), channel_id=1, source_target_pairs={{0,4},{4,8},{8,12},{12,0},{1,5},{5,9},{9,13},{13,1},{2,6},{6,10},{... | collective-permute-start | bytes 786440 | tf_op jit(solution)/shard_map/pages_over_y/ppermute | solution.py:272
  22.2 4.5 %collective-permute-start.1 = (bf16[2,2,256,128]{3,2,1,0:T(8,128)(2,1)S(1)}, bf16[2,2,256,128]{3,2,1,0:T(8,128)(2,1)S(1)}, u32[]{:S(2)}, u32[]{:S(2)}) collective-permute-start(bf16[2,2,256,128]{3,2,1,0:T(8,128)(2,1)S(1)} %get-tuple-element.13), channel_id=1, source_target_pairs={{0,8},{4,12},{8,0},{12,4},{1,9},{5,13},{9,1},{13,5},{2,10},{6,14},... | collective-permute-start | bytes 786440 | tf_op jit(solution)/shard_map/pages_over_y/ppermute | solution.py:272
  26.7 3.0 %collective-permute-start.2 = (bf16[2,2,256,128]{3,2,1,0:T(8,128)(2,1)S(1)}, bf16[2,2,256,128]{3,2,1,0:T(8,128)(2,1)S(1)}, u32[]{:S(2)}, u32[]{:S(2)}) collective-permute-start(bf16[2,2,256,128]{3,2,1,0:T(8,128)(2,1)S(1)} %get-tuple-element.14), channel_id=1, source_target_pairs={{0,12},{4,0},{8,4},{12,8},{1,13},{5,1},{9,5},{13,9},{2,14},{6,2},{... | collective-permute-start | bytes 786440 | tf_op jit(solution)/shard_map/pages_over_y/ppermute | solution.py:272
  29.7 0.0 all-to-all-done.x_ref
  29.7 0.1 queries_over_mp.1
  29.8 0.0 copy-start.4
  29.8 0.0 copy-start.5
  29.8 0.0 copy-start.6
  29.8 11.0 %all_to_all.25.refs_0_ = bf16[16,2,16,128]{3,2,1,0:T(8,128)(2,1)S(1)} all-to-all(bf16[16,2,16,128]{3,2,1,0:T(8,128)(2,1)S(1)} %queries_over_mp.1), channel_id=1, replica_groups=mesh['zo'=8,'zn'=2,'c'=2,'y'=4,'x'=4] {'y','x'}, dimensions={0} | all-to-all | bytes 262144 | tf_op jit(solution)/shard_map/queries_over_mp/all_to_all | solution.py:34
  40.9 0.0 collective-permute-done.refs_2_
  40.9 0.0 collective-permute-done.1.refs_3_
  40.9 0.0 collective-permute-done.2.refs_4_
  40.9 0.0 copy-done.4
  40.9 0.0 copy-done.5
  40.9 0.0 copy-done.6
  40.9 1.5 %attention.1 = (bf16[16,40,128]{2,1,0:T(8,128)(2,1)S(1)}, s32[32,128]{1,0:T(8,128)S(1)}) custom-call(bf16[16,2,16,128]{3,2,1,0:T(8,128)(2,1)S(1)} %all_to_all.25.refs_0_, bf16[2,2,256,128]{3,2,1,0:T(8,128)(2,1)S(1)} %get-tuple-element.11.refs_1_, bf16[2,2,256,128]{3,2,1,0:T(8,128)(2,1)S(1)} %collective-permute-done.refs_2_, ...), custom_call_target="tpu_custom_call" | custom-call | tf_op jit(solution)/shard_map/attention/pallas_call | solution.py:40
  42.4 12.5 %all_to_all.26.x_ref = bf16[16,40,128]{2,1,0:T(8,128)(2,1)S(1)} all-to-all(bf16[16,40,128]{2,1,0:T(8,128)(2,1)S(1)} %get-tuple-element.15), channel_id=1, replica_groups=mesh['zo'=8,'zn'=2,'c'=2,'y'=4,'x'=4] {'zn','c','x'}, dimensions={0} | all-to-all | bytes 327680 | tf_op jit(solution)/shard_map/merge/all_to_all | solution.py:34
  54.9 0.5 merge.2
  55.3 14.8 %all_to_all.27.x_ref = bf16[8,40,128]{2,1,0:T(8,128)(2,1)S(1)} all-to-all(bf16[8,40,128]{2,1,0:T(8,128)(2,1)S(1)} %merge.2), channel_id=1, replica_groups={{192,256,320,384,448,0,64,128},{193,257,321,385,449,1,65,129},{194,258,..., dimensions={0} | all-to-all | bytes 163840 | tf_op jit(solution)/shard_map/merge/all_to_all | solution.py:34
  70.1 0.3 merge.3
  70.4 6.7 %all-gather = bf16[128,128]{1,0:T(8,128)(2,1)S(1)} all-gather(bf16[32,128]{1,0:T(8,128)(2,1)S(1)} %merge.3), channel_id=2, replica_groups=mesh['zo'=8,'zn'=2,'c'=2,'y'=4,'x'=4] {'zn','c'}, dimensions={0}, use_global_device_ids=true | all-gather | bytes 40960 | tf_op jit(solution)/shard_map/merge/all_gather | solution.py:295
  77.1 0.0 copy-done.1
  77.1 0.0 copy-done.2
  77.1 0.0 copy-done.3
  77.1 0.5 projection.2
  77.6 9.5 %all_to_all.28.x_ref = bf16[16,4,128]{2,1,0:T(4,128)(2,1)S(1)} all-to-all(bf16[16,4,128]{2,1,0:T(4,128)(2,1)S(1)} %projection.2), channel_id=1, replica_groups=mesh['zo'=8,'zn'=2,'c'=2,'y'=4,'x'=4] {'y','x'}, dimensions={0} | all-to-all | bytes 32768 | tf_op jit(solution)/shard_map/projection/all_to_all | solution.py:34
  87.1 0.6 projection.3
  (5 shorter events, 0.0 us)
Async XLA Ops:
  0.0 0.7 copy-start.7
  0.7 17.7 %copy-start = (bf16[32,8,8,256]{3,2,1,0:T(8,128)(2,1)S(1)}, bf16[32,8,8,256]{3,2,1,0:T(8,128)(2,1)}, u32[]{:S(2)}) copy-start(bf16[32,8,8,256]{3,2,1,0:T(8,128)(2,1)} %kv_ref.1) | copy-start | bytes 3145732
  1.4 28.2 %all-to-all-start = ((bf16[32,4,128]{2,1,0:T(4,128)(2,1)}), bf16[32,4,128]{2,1,0:T(4,128)(2,1)S(1)}, u32[]{:S(2)}, u32[]{:S(2)}) async-start(bf16[32,4,128]{2,1,0:T(4,128)(2,1)} %queries_over_kv.1), calls=%async_computation | async-start | bytes 65536 | tf_op jit(solution)/shard_map/queries_over_kv/all_to_all | solution.py:34
  18.9 21.9 %collective-permute-start = (bf16[2,2,256,128]{3,2,1,0:T(8,128)(2,1)S(1)}, bf16[2,2,256,128]{3,2,1,0:T(8,128)(2,1)S(1)}, u32[]{:S(2)}, u32[]{:S(2)}) collective-permute-start(bf16[2,2,256,128]{3,2,1,0:T(8,128)(2,1)S(1)} %get-tuple-element.12), channel_id=1, source_target_pairs={{0,4},{4,8},{8,12},{12,0},{1,5},{5,9},{9,13},{13,1},{2,6},{6,10},{... | collective-permute-start | bytes 786440 | tf_op jit(solution)/shard_map/pages_over_y/ppermute | solution.py:272
  22.2 18.7 %collective-permute-start.1 = (bf16[2,2,256,128]{3,2,1,0:T(8,128)(2,1)S(1)}, bf16[2,2,256,128]{3,2,1,0:T(8,128)(2,1)S(1)}, u32[]{:S(2)}, u32[]{:S(2)}) collective-permute-start(bf16[2,2,256,128]{3,2,1,0:T(8,128)(2,1)S(1)} %get-tuple-element.13), channel_id=1, source_target_pairs={{0,8},{4,12},{8,0},{12,4},{1,9},{5,13},{9,1},{13,5},{2,10},{6,14},... | collective-permute-start | bytes 786440 | tf_op jit(solution)/shard_map/pages_over_y/ppermute | solution.py:272
  26.7 14.2 %collective-permute-start.2 = (bf16[2,2,256,128]{3,2,1,0:T(8,128)(2,1)S(1)}, bf16[2,2,256,128]{3,2,1,0:T(8,128)(2,1)S(1)}, u32[]{:S(2)}, u32[]{:S(2)}) collective-permute-start(bf16[2,2,256,128]{3,2,1,0:T(8,128)(2,1)S(1)} %get-tuple-element.14), channel_id=1, source_target_pairs={{0,12},{4,0},{8,4},{12,8},{1,13},{5,1},{9,5},{13,9},{2,14},{6,2},{... | collective-permute-start | bytes 786440 | tf_op jit(solution)/shard_map/pages_over_y/ppermute | solution.py:272
  29.8 11.1 %copy-start.4 = (s32[32,32]{1,0:T(8,128)S(1)}, s32[32,32]{1,0:T(8,128)}, u32[]{:S(2)}) copy-start(s32[32,32]{1,0:T(8,128)} %refs_5_.1) | copy-start | bytes 12292
  29.8 11.1 %copy-start.5 = (s32[32]{0:T(128)S(1)}, s32[32]{0:T(128)}, u32[]{:S(2)}) copy-start(s32[32]{0:T(128)} %refs_6_.1) | copy-start | bytes 388
  29.8 11.1 %copy-start.6 = (s32[32]{0:T(128)S(1)}, s32[32]{0:T(128)}, u32[]{:S(2)}) copy-start(s32[32]{0:T(128)} %refs_7_.1) | copy-start | bytes 388
  40.9 36.2 %copy-start.1 = (bf16[512,1024]{1,0:T(8,128)(2,1)S(1)}, bf16[512,1024]{1,0:T(8,128)(2,1)}, u32[]{:S(2)}) copy-start(bf16[512,1024]{1,0:T(8,128)(2,1)} %down_ref.1) | copy-start | bytes 3145732
  42.4 34.7 %copy-start.2 = (bf16[1024,256]{1,0:T(8,128)(2,1)S(1)}, bf16[1024,256]{1,0:T(8,128)(2,1)}, u32[]{:S(2)}) copy-start(bf16[1024,256]{1,0:T(8,128)(2,1)} %up_ref.1) | copy-start | bytes 1572868
  54.9 22.2 %copy-start.3 = (bf16[512,256]{1,0:T(8,128)(2,1)S(1)}, bf16[512,256]{1,0:T(8,128)(2,1)}, u32[]{:S(2)}) copy-start(bf16[512,256]{1,0:T(8,128)(2,1)} %weight_ref.1) | copy-start | bytes 786436

commit v6 on v5

--- a/solution.py
+++ b/solution.py
@@ -68,8 +68,8 @@
     y = lax.axis_index("y")
     for k in range(parts):
         wide = kv_ref[pages * k : pages * k + pages].astype(f32).reshape(8 * tokens, 256)
-        wide_ref[0] = wide[:, :128]
-        wide_ref[1] = wide[:, 128:]
+        wide_ref[0, : 8 * tokens] = wide[:, :128]
+        wide_ref[1, : 8 * tokens] = wide[:, 128:]
         for step, piece_ref in enumerate(piece_refs):
             for head in range(2):
                 first = 2 * lax.rem(y + step, 4) + head
@@ -264,7 +264,7 @@
             sort_pages,
             (shape((2, 2, tokens, row // 2), bf16),) * 4,
             key_value_pages,
-            scratch=[pltpu.VMEM((2, tokens // 4 * kv_heads, row // 2), f32)],
+            scratch=[pltpu.VMEM((2, (tokens // 4 + 1) * kv_heads, row // 2), f32)],
         )
         pieces = list(pieces)
         for step in range(1, 4):

time: 88.2 us -> 88.2 us (level)
  no operation moved by 1% of the time
where the time goes in v6:
time: 88.2 us; the launch traced here: 87.7 us
  blocking collectives  54.4 us (62%)
  starting transfers between devices  27.7 us (31%)
  Pallas kernels  4.81 us (5%)
    all_to_all x4, blocking collectives, exchange(): lax.all_to_all(value, axes, split_axis=0, concat_axis=0, tiled=True, axis...  47.7 us
    all_to_all x1, starting transfers between devices, exchange(): lax.all_to_all(value, axes, split_axis=0, concat_axis=0, tiled=True, axis...  17 us
    ppermute x3, starting transfers between devices, on_device(): pieces[step] = lax.ppermute(pieces[step], 'y', ring)  10.7 us
    all_gather x1, blocking collectives, on_device(): attended = lax.all_gather(attended, NEAR)  6.67 us
    pallas_call x8, Pallas kernels, call(): pl.pallas_call(kernel, out_shape=out_shape, in_specs=[pl.BlockSpec(memory...  4.81 us
  transfers between devices with their start and end apart: 4, of which 0 were waited for; matrix products, arithmetic and copies ran while one was open for 0% of the time, Pallas kernels for 1%

profile of v6, /device:TPU:1, one launch (start us, length us, event | category | flops | bytes accessed | tf_op | source)
XLA Modules:
  0.0 87.7 jit_solution(190257770151143869)
XLA Ops:
  0.0 0.7 copy-done.7
  0.7 0.7 queries_over_kv.1
  1.4 17.0 %all-to-all-start = ((bf16[32,4,128]{2,1,0:T(4,128)(2,1)}), bf16[32,4,128]{2,1,0:T(4,128)(2,1)S(1)}, u32[]{:S(2)}, u32[]{:S(2)}) async-start(bf16[32,4,128]{2,1,0:T(4,128)(2,1)} %queries_over_kv.1), calls=%async_computation | async-start | bytes 65536 | tf_op jit(solution)/shard_map/queries_over_kv/all_to_all | solution.py:34
  18.4 0.0 copy-done
  18.4 0.5 pages_over_y.1
  19.0 3.2 %collective-permute-start = (bf16[2,2,256,128]{3,2,1,0:T(8,128)(2,1)S(1)}, bf16[2,2,256,128]{3,2,1,0:T(8,128)(2,1)S(1)}, u32[]{:S(2)}, u32[]{:S(2)}) collective-permute-start(bf16[2,2,256,128]{3,2,1,0:T(8,128)(2,1)S(1)} %get-tuple-element.12), channel_id=1, source_target_pairs={{0,4},{4,8},{8,12},{12,0},{1,5},{5,9},{9,13},{13,1},{2,6},{6,10},{... | collective-permute-start | bytes 786440 | tf_op jit(solution)/shard_map/pages_over_y/ppermute | solution.py:272
  22.2 4.5 %collective-permute-start.1 = (bf16[2,2,256,128]{3,2,1,0:T(8,128)(2,1)S(1)}, bf16[2,2,256,128]{3,2,1,0:T(8,128)(2,1)S(1)}, u32[]{:S(2)}, u32[]{:S(2)}) collective-permute-start(bf16[2,2,256,128]{3,2,1,0:T(8,128)(2,1)S(1)} %get-tuple-element.13), channel_id=1, source_target_pairs={{0,8},{4,12},{8,0},{12,4},{1,9},{5,13},{9,1},{13,5},{2,10},{6,14},... | collective-permute-start | bytes 786440 | tf_op jit(solution)/shard_map/pages_over_y/ppermute | solution.py:272
  26.7 3.0 %collective-permute-start.2 = (bf16[2,2,256,128]{3,2,1,0:T(8,128)(2,1)S(1)}, bf16[2,2,256,128]{3,2,1,0:T(8,128)(2,1)S(1)}, u32[]{:S(2)}, u32[]{:S(2)}) collective-permute-start(bf16[2,2,256,128]{3,2,1,0:T(8,128)(2,1)S(1)} %get-tuple-element.14), channel_id=1, source_target_pairs={{0,12},{4,0},{8,4},{12,8},{1,13},{5,1},{9,5},{13,9},{2,14},{6,2},{... | collective-permute-start | bytes 786440 | tf_op jit(solution)/shard_map/pages_over_y/ppermute | solution.py:272
  29.7 0.0 all-to-all-done.x_ref
  29.7 0.1 queries_over_mp.1
  29.8 0.0 copy-start.4
  29.8 0.0 copy-start.5
  29.8 0.0 copy-start.6
  29.8 11.0 %all_to_all.25.refs_0_ = bf16[16,2,16,128]{3,2,1,0:T(8,128)(2,1)S(1)} all-to-all(bf16[16,2,16,128]{3,2,1,0:T(8,128)(2,1)S(1)} %queries_over_mp.1), channel_id=1, replica_groups=mesh['zo'=8,'zn'=2,'c'=2,'y'=4,'x'=4] {'y','x'}, dimensions={0} | all-to-all | bytes 262144 | tf_op jit(solution)/shard_map/queries_over_mp/all_to_all | solution.py:34
  40.9 0.0 collective-permute-done.refs_2_
  40.9 0.0 collective-permute-done.1.refs_3_
  40.9 0.0 collective-permute-done.2.refs_4_
  40.9 0.0 copy-done.4
  40.9 0.0 copy-done.5
  40.9 0.0 copy-done.6
  40.9 1.5 %attention.1 = (bf16[16,40,128]{2,1,0:T(8,128)(2,1)S(1)}, s32[32,128]{1,0:T(8,128)S(1)}) custom-call(bf16[16,2,16,128]{3,2,1,0:T(8,128)(2,1)S(1)} %all_to_all.25.refs_0_, bf16[2,2,256,128]{3,2,1,0:T(8,128)(2,1)S(1)} %get-tuple-element.11.refs_1_, bf16[2,2,256,128]{3,2,1,0:T(8,128)(2,1)S(1)} %collective-permute-done.refs_2_, ...), custom_call_target="tpu_custom_call" | custom-call | tf_op jit(solution)/shard_map/attention/pallas_call | solution.py:40
  42.4 12.5 %all_to_all.26.x_ref = bf16[16,40,128]{2,1,0:T(8,128)(2,1)S(1)} all-to-all(bf16[16,40,128]{2,1,0:T(8,128)(2,1)S(1)} %get-tuple-element.15), channel_id=1, replica_groups=mesh['zo'=8,'zn'=2,'c'=2,'y'=4,'x'=4] {'zn','c','x'}, dimensions={0} | all-to-all | bytes 327680 | tf_op jit(solution)/shard_map/merge/all_to_all | solution.py:34
  54.9 0.5 merge.2
  55.3 14.8 %all_to_all.27.x_ref = bf16[8,40,128]{2,1,0:T(8,128)(2,1)S(1)} all-to-all(bf16[8,40,128]{2,1,0:T(8,128)(2,1)S(1)} %merge.2), channel_id=1, replica_groups={{192,256,320,384,448,0,64,128},{193,257,321,385,449,1,65,129},{194,258,..., dimensions={0} | all-to-all | bytes 163840 | tf_op jit(solution)/shard_map/merge/all_to_all | solution.py:34
  70.1 0.3 merge.3
  70.4 6.7 %all-gather = bf16[128,128]{1,0:T(8,128)(2,1)S(1)} all-gather(bf16[32,128]{1,0:T(8,128)(2,1)S(1)} %merge.3), channel_id=2, replica_groups=mesh['zo'=8,'zn'=2,'c'=2,'y'=4,'x'=4] {'zn','c'}, dimensions={0}, use_global_device_ids=true | all-gather | bytes 40960 | tf_op jit(solution)/shard_map/merge/all_gather | solution.py:295
  77.1 0.0 copy-done.1
  77.1 0.0 copy-done.2
  77.1 0.0 copy-done.3
  77.1 0.5 projection.2
  77.6 9.5 %all_to_all.28.x_ref = bf16[16,4,128]{2,1,0:T(4,128)(2,1)S(1)} all-to-all(bf16[16,4,128]{2,1,0:T(4,128)(2,1)S(1)} %projection.2), channel_id=1, replica_groups=mesh['zo'=8,'zn'=2,'c'=2,'y'=4,'x'=4] {'y','x'}, dimensions={0} | all-to-all | bytes 32768 | tf_op jit(solution)/shard_map/projection/all_to_all | solution.py:34
  87.1 0.6 projection.3
  (5 shorter events, 0.0 us)
Async XLA Ops:
  0.0 0.7 copy-start.7
  0.7 17.7 %copy-start = (bf16[32,8,8,256]{3,2,1,0:T(8,128)(2,1)S(1)}, bf16[32,8,8,256]{3,2,1,0:T(8,128)(2,1)}, u32[]{:S(2)}) copy-start(bf16[32,8,8,256]{3,2,1,0:T(8,128)(2,1)} %kv_ref.1) | copy-start | bytes 3145732
  1.4 28.3 %all-to-all-start = ((bf16[32,4,128]{2,1,0:T(4,128)(2,1)}), bf16[32,4,128]{2,1,0:T(4,128)(2,1)S(1)}, u32[]{:S(2)}, u32[]{:S(2)}) async-start(bf16[32,4,128]{2,1,0:T(4,128)(2,1)} %queries_over_kv.1), calls=%async_computation | async-start | bytes 65536 | tf_op jit(solution)/shard_map/queries_over_kv/all_to_all | solution.py:34
  19.0 21.9 %collective-permute-start = (bf16[2,2,256,128]{3,2,1,0:T(8,128)(2,1)S(1)}, bf16[2,2,256,128]{3,2,1,0:T(8,128)(2,1)S(1)}, u32[]{:S(2)}, u32[]{:S(2)}) collective-permute-start(bf16[2,2,256,128]{3,2,1,0:T(8,128)(2,1)S(1)} %get-tuple-element.12), channel_id=1, source_target_pairs={{0,4},{4,8},{8,12},{12,0},{1,5},{5,9},{9,13},{13,1},{2,6},{6,10},{... | collective-permute-start | bytes 786440 | tf_op jit(solution)/shard_map/pages_over_y/ppermute | solution.py:272
  22.2 18.7 %collective-permute-start.1 = (bf16[2,2,256,128]{3,2,1,0:T(8,128)(2,1)S(1)}, bf16[2,2,256,128]{3,2,1,0:T(8,128)(2,1)S(1)}, u32[]{:S(2)}, u32[]{:S(2)}) collective-permute-start(bf16[2,2,256,128]{3,2,1,0:T(8,128)(2,1)S(1)} %get-tuple-element.13), channel_id=1, source_target_pairs={{0,8},{4,12},{8,0},{12,4},{1,9},{5,13},{9,1},{13,5},{2,10},{6,14},... | collective-permute-start | bytes 786440 | tf_op jit(solution)/shard_map/pages_over_y/ppermute | solution.py:272
  26.7 14.2 %collective-permute-start.2 = (bf16[2,2,256,128]{3,2,1,0:T(8,128)(2,1)S(1)}, bf16[2,2,256,128]{3,2,1,0:T(8,128)(2,1)S(1)}, u32[]{:S(2)}, u32[]{:S(2)}) collective-permute-start(bf16[2,2,256,128]{3,2,1,0:T(8,128)(2,1)S(1)} %get-tuple-element.14), channel_id=1, source_target_pairs={{0,12},{4,0},{8,4},{12,8},{1,13},{5,1},{9,5},{13,9},{2,14},{6,2},{... | collective-permute-start | bytes 786440 | tf_op jit(solution)/shard_map/pages_over_y/ppermute | solution.py:272
  29.8 11.1 %copy-start.4 = (s32[32,32]{1,0:T(8,128)S(1)}, s32[32,32]{1,0:T(8,128)}, u32[]{:S(2)}) copy-start(s32[32,32]{1,0:T(8,128)} %refs_5_.1) | copy-start | bytes 12292
  29.8 11.1 %copy-start.5 = (s32[32]{0:T(128)S(1)}, s32[32]{0:T(128)}, u32[]{:S(2)}) copy-start(s32[32]{0:T(128)} %refs_6_.1) | copy-start | bytes 388
  29.8 11.1 %copy-start.6 = (s32[32]{0:T(128)S(1)}, s32[32]{0:T(128)}, u32[]{:S(2)}) copy-start(s32[32]{0:T(128)} %refs_7_.1) | copy-start | bytes 388
  40.9 36.2 %copy-start.1 = (bf16[512,1024]{1,0:T(8,128)(2,1)S(1)}, bf16[512,1024]{1,0:T(8,128)(2,1)}, u32[]{:S(2)}) copy-start(bf16[512,1024]{1,0:T(8,128)(2,1)} %down_ref.1) | copy-start | bytes 3145732
  42.4 34.7 %copy-start.2 = (bf16[1024,256]{1,0:T(8,128)(2,1)S(1)}, bf16[1024,256]{1,0:T(8,128)(2,1)}, u32[]{:S(2)}) copy-start(bf16[1024,256]{1,0:T(8,128)(2,1)} %up_ref.1) | copy-start | bytes 1572868
  54.9 22.2 %copy-start.3 = (bf16[512,256]{1,0:T(8,128)(2,1)S(1)}, bf16[512,256]{1,0:T(8,128)(2,1)}, u32[]{:S(2)}) copy-start(bf16[512,256]{1,0:T(8,128)(2,1)} %weight_ref.1) | copy-start | bytes 786436

commit v7 on v6

--- a/solution.py
+++ b/solution.py
@@ -26,6 +26,9 @@
 
 QUERY_FIRST = 24
 MERGE_FIRST = 3
+QUERY_ORDER = sorted(
+    range(32), key=lambda k: (k != QUERY_FIRST, abs((k - QUERY_FIRST + 16) % 32 - 16) // 2 * -1, k)
+)
 
 
 def exchange(value, axes, first=0):
@@ -95,7 +98,8 @@
 
 def regroup_queries(x_ref, out_ref):
     x = x_ref[...].astype(f32)
-    x = jnp.concatenate([x[32 - QUERY_FIRST :], x[: 32 - QUERY_FIRST]], axis=0)
+    places = [QUERY_ORDER.index(k) for k in range(32)]
+    x = jnp.concatenate([x[place : place + 1] for place in places], axis=0)
     x = x.reshape(8, 4, 4, 128)
     group = lax.broadcasted_iota(i32, (32, 128), 1) // 32
     blocks = [x[:, i].reshape(32, 128) for i in range(4)]
@@ -257,7 +261,9 @@
             queries.T,
             cost=pl.CostEstimate(flops=10**10, bytes_accessed=10**7, transcendentals=0),
         )
-        spread = exchange(packed, KV, QUERY_FIRST)
+        spread = lax.all_to_all(
+            packed, KV, split_axis=0, concat_axis=0, tiled=True, axis_index_groups=[QUERY_ORDER]
+        )
     with jax.named_scope("pages_over_y"):
         tokens = pages_here * slice_tokens
         pieces = call(

time: 88.2 us -> 88.2 us (level)
  no operation moved by 1% of the time
where the time goes in v7:
time: 88.2 us; the launch traced here: 87.7 us
  blocking collectives  54.4 us (62%)
  starting transfers between devices  27.7 us (31%)
  Pallas kernels  4.81 us (5%)
    all_to_all x4, blocking collectives, exchange(): lax.all_to_all(value, axes, split_axis=0, concat_axis=0, tiled=True, axis...  47.7 us
    all_to_all x1, starting transfers between devices, on_device(): lax.all_to_all(packed, KV, split_axis=0, concat_axis=0, tiled=True, axis_...  17 us
    ppermute x3, starting transfers between devices, on_device(): pieces[step] = lax.ppermute(pieces[step], 'y', ring)  10.7 us
    all_gather x1, blocking collectives, on_device(): attended = lax.all_gather(attended, NEAR)  6.67 us
    pallas_call x8, Pallas kernels, call(): pl.pallas_call(kernel, out_shape=out_shape, in_specs=[pl.BlockSpec(memory...  4.81 us
  transfers between devices with their start and end apart: 4, of which 0 were waited for; matrix products, arithmetic and copies ran while one was open for 0% of the time, Pallas kernels for 1%

profile of v7, /device:TPU:1, one launch (start us, length us, event | category | flops | bytes accessed | tf_op | source)
XLA Modules:
  0.0 87.7 jit_solution(14282860077619042958)
XLA Ops:
  0.0 0.7 copy-done.7
  0.7 0.7 queries_over_kv.1
  1.4 17.0 %all-to-all-start = ((bf16[32,4,128]{2,1,0:T(4,128)(2,1)}), bf16[32,4,128]{2,1,0:T(4,128)(2,1)S(1)}, u32[]{:S(2)}, u32[]{:S(2)}) async-start(bf16[32,4,128]{2,1,0:T(4,128)(2,1)} %queries_over_kv.1), calls=%async_computation | async-start | bytes 65536 | tf_op jit(solution)/shard_map/queries_over_kv/all_to_all | solution.py:264
  18.4 0.0 copy-done
  18.4 0.5 pages_over_y.1
  19.0 3.2 %collective-permute-start = (bf16[2,2,256,128]{3,2,1,0:T(8,128)(2,1)S(1)}, bf16[2,2,256,128]{3,2,1,0:T(8,128)(2,1)S(1)}, u32[]{:S(2)}, u32[]{:S(2)}) collective-permute-start(bf16[2,2,256,128]{3,2,1,0:T(8,128)(2,1)S(1)} %get-tuple-element.12), channel_id=1, source_target_pairs={{0,4},{4,8},{8,12},{12,0},{1,5},{5,9},{9,13},{13,1},{2,6},{6,10},{... | collective-permute-start | bytes 786440 | tf_op jit(solution)/shard_map/pages_over_y/ppermute | solution.py:278
  22.2 4.5 %collective-permute-start.1 = (bf16[2,2,256,128]{3,2,1,0:T(8,128)(2,1)S(1)}, bf16[2,2,256,128]{3,2,1,0:T(8,128)(2,1)S(1)}, u32[]{:S(2)}, u32[]{:S(2)}) collective-permute-start(bf16[2,2,256,128]{3,2,1,0:T(8,128)(2,1)S(1)} %get-tuple-element.13), channel_id=1, source_target_pairs={{0,8},{4,12},{8,0},{12,4},{1,9},{5,13},{9,1},{13,5},{2,10},{6,14},... | collective-permute-start | bytes 786440 | tf_op jit(solution)/shard_map/pages_over_y/ppermute | solution.py:278
  26.7 3.0 %collective-permute-start.2 = (bf16[2,2,256,128]{3,2,1,0:T(8,128)(2,1)S(1)}, bf16[2,2,256,128]{3,2,1,0:T(8,128)(2,1)S(1)}, u32[]{:S(2)}, u32[]{:S(2)}) collective-permute-start(bf16[2,2,256,128]{3,2,1,0:T(8,128)(2,1)S(1)} %get-tuple-element.14), channel_id=1, source_target_pairs={{0,12},{4,0},{8,4},{12,8},{1,13},{5,1},{9,5},{13,9},{2,14},{6,2},{... | collective-permute-start | bytes 786440 | tf_op jit(solution)/shard_map/pages_over_y/ppermute | solution.py:278
  29.7 0.0 all-to-all-done.x_ref
  29.7 0.1 queries_over_mp.1
  29.8 0.0 copy-start.4
  29.8 0.0 copy-start.5
  29.8 0.0 copy-start.6
  29.9 11.0 %all_to_all.25.refs_0_ = bf16[16,2,16,128]{3,2,1,0:T(8,128)(2,1)S(1)} all-to-all(bf16[16,2,16,128]{3,2,1,0:T(8,128)(2,1)S(1)} %queries_over_mp.1), channel_id=1, replica_groups=mesh['zo'=8,'zn'=2,'c'=2,'y'=4,'x'=4] {'y','x'}, dimensions={0} | all-to-all | bytes 262144 | tf_op jit(solution)/shard_map/queries_over_mp/all_to_all | solution.py:37
  40.9 0.0 collective-permute-done.refs_2_
  40.9 0.0 collective-permute-done.1.refs_3_
  40.9 0.0 collective-permute-done.2.refs_4_
  40.9 0.0 copy-done.4
  40.9 0.0 copy-done.5
  40.9 0.0 copy-done.6
  40.9 1.5 %attention.1 = (bf16[16,40,128]{2,1,0:T(8,128)(2,1)S(1)}, s32[32,128]{1,0:T(8,128)S(1)}) custom-call(bf16[16,2,16,128]{3,2,1,0:T(8,128)(2,1)S(1)} %all_to_all.25.refs_0_, bf16[2,2,256,128]{3,2,1,0:T(8,128)(2,1)S(1)} %get-tuple-element.11.refs_1_, bf16[2,2,256,128]{3,2,1,0:T(8,128)(2,1)S(1)} %collective-permute-done.refs_2_, ...), custom_call_target="tpu_custom_call" | custom-call | tf_op jit(solution)/shard_map/attention/pallas_call | solution.py:43
  42.4 12.5 %all_to_all.26.x_ref = bf16[16,40,128]{2,1,0:T(8,128)(2,1)S(1)} all-to-all(bf16[16,40,128]{2,1,0:T(8,128)(2,1)S(1)} %get-tuple-element.15), channel_id=1, replica_groups=mesh['zo'=8,'zn'=2,'c'=2,'y'=4,'x'=4] {'zn','c','x'}, dimensions={0} | all-to-all | bytes 327680 | tf_op jit(solution)/shard_map/merge/all_to_all | solution.py:37
  54.9 0.5 merge.2
  55.3 14.6 %all_to_all.27.x_ref = bf16[8,40,128]{2,1,0:T(8,128)(2,1)S(1)} all-to-all(bf16[8,40,128]{2,1,0:T(8,128)(2,1)S(1)} %merge.2), channel_id=1, replica_groups={{192,256,320,384,448,0,64,128},{193,257,321,385,449,1,65,129},{194,258,..., dimensions={0} | all-to-all | bytes 163840 | tf_op jit(solution)/shard_map/merge/all_to_all | solution.py:37
  70.0 0.3 merge.3
  70.3 6.7 %all-gather = bf16[128,128]{1,0:T(8,128)(2,1)S(1)} all-gather(bf16[32,128]{1,0:T(8,128)(2,1)S(1)} %merge.3), channel_id=2, replica_groups=mesh['zo'=8,'zn'=2,'c'=2,'y'=4,'x'=4] {'zn','c'}, dimensions={0}, use_global_device_ids=true | all-gather | bytes 40960 | tf_op jit(solution)/shard_map/merge/all_gather | solution.py:301
  77.0 0.0 copy-done.1
  77.0 0.0 copy-done.2
  77.0 0.0 copy-done.3
  77.0 0.5 projection.2
  77.5 9.6 %all_to_all.28.x_ref = bf16[16,4,128]{2,1,0:T(4,128)(2,1)S(1)} all-to-all(bf16[16,4,128]{2,1,0:T(4,128)(2,1)S(1)} %projection.2), channel_id=1, replica_groups=mesh['zo'=8,'zn'=2,'c'=2,'y'=4,'x'=4] {'y','x'}, dimensions={0} | all-to-all | bytes 32768 | tf_op jit(solution)/shard_map/projection/all_to_all | solution.py:37
  87.1 0.6 projection.3
  (5 shorter events, 0.0 us)
Async XLA Ops:
  0.0 0.7 copy-start.7
  0.7 17.7 %copy-start = (bf16[32,8,8,256]{3,2,1,0:T(8,128)(2,1)S(1)}, bf16[32,8,8,256]{3,2,1,0:T(8,128)(2,1)}, u32[]{:S(2)}) copy-start(bf16[32,8,8,256]{3,2,1,0:T(8,128)(2,1)} %kv_ref.1) | copy-start | bytes 3145732
  1.4 28.3 %all-to-all-start = ((bf16[32,4,128]{2,1,0:T(4,128)(2,1)}), bf16[32,4,128]{2,1,0:T(4,128)(2,1)S(1)}, u32[]{:S(2)}, u32[]{:S(2)}) async-start(bf16[32,4,128]{2,1,0:T(4,128)(2,1)} %queries_over_kv.1), calls=%async_computation | async-start | bytes 65536 | tf_op jit(solution)/shard_map/queries_over_kv/all_to_all | solution.py:264
  19.0 21.9 %collective-permute-start = (bf16[2,2,256,128]{3,2,1,0:T(8,128)(2,1)S(1)}, bf16[2,2,256,128]{3,2,1,0:T(8,128)(2,1)S(1)}, u32[]{:S(2)}, u32[]{:S(2)}) collective-permute-start(bf16[2,2,256,128]{3,2,1,0:T(8,128)(2,1)S(1)} %get-tuple-element.12), channel_id=1, source_target_pairs={{0,4},{4,8},{8,12},{12,0},{1,5},{5,9},{9,13},{13,1},{2,6},{6,10},{... | collective-permute-start | bytes 786440 | tf_op jit(solution)/shard_map/pages_over_y/ppermute | solution.py:278
  22.2 18.7 %collective-permute-start.1 = (bf16[2,2,256,128]{3,2,1,0:T(8,128)(2,1)S(1)}, bf16[2,2,256,128]{3,2,1,0:T(8,128)(2,1)S(1)}, u32[]{:S(2)}, u32[]{:S(2)}) collective-permute-start(bf16[2,2,256,128]{3,2,1,0:T(8,128)(2,1)S(1)} %get-tuple-element.13), channel_id=1, source_target_pairs={{0,8},{4,12},{8,0},{12,4},{1,9},{5,13},{9,1},{13,5},{2,10},{6,14},... | collective-permute-start | bytes 786440 | tf_op jit(solution)/shard_map/pages_over_y/ppermute | solution.py:278
  26.7 14.2 %collective-permute-start.2 = (bf16[2,2,256,128]{3,2,1,0:T(8,128)(2,1)S(1)}, bf16[2,2,256,128]{3,2,1,0:T(8,128)(2,1)S(1)}, u32[]{:S(2)}, u32[]{:S(2)}) collective-permute-start(bf16[2,2,256,128]{3,2,1,0:T(8,128)(2,1)S(1)} %get-tuple-element.14), channel_id=1, source_target_pairs={{0,12},{4,0},{8,4},{12,8},{1,13},{5,1},{9,5},{13,9},{2,14},{6,2},{... | collective-permute-start | bytes 786440 | tf_op jit(solution)/shard_map/pages_over_y/ppermute | solution.py:278
  29.8 11.1 %copy-start.4 = (s32[32,32]{1,0:T(8,128)S(1)}, s32[32,32]{1,0:T(8,128)}, u32[]{:S(2)}) copy-start(s32[32,32]{1,0:T(8,128)} %refs_5_.1) | copy-start | bytes 12292
  29.8 11.1 %copy-start.5 = (s32[32]{0:T(128)S(1)}, s32[32]{0:T(128)}, u32[]{:S(2)}) copy-start(s32[32]{0:T(128)} %refs_6_.1) | copy-start | bytes 388
  29.8 11.1 %copy-start.6 = (s32[32]{0:T(128)S(1)}, s32[32]{0:T(128)}, u32[]{:S(2)}) copy-start(s32[32]{0:T(128)} %refs_7_.1) | copy-start | bytes 388
  40.9 36.1 %copy-start.1 = (bf16[512,1024]{1,0:T(8,128)(2,1)S(1)}, bf16[512,1024]{1,0:T(8,128)(2,1)}, u32[]{:S(2)}) copy-start(bf16[512,1024]{1,0:T(8,128)(2,1)} %down_ref.1) | copy-start | bytes 3145732
  42.4 34.6 %copy-start.2 = (bf16[1024,256]{1,0:T(8,128)(2,1)S(1)}, bf16[1024,256]{1,0:T(8,128)(2,1)}, u32[]{:S(2)}) copy-start(bf16[1024,256]{1,0:T(8,128)(2,1)} %up_ref.1) | copy-start | bytes 1572868
  54.9 22.1 %copy-start.3 = (bf16[512,256]{1,0:T(8,128)(2,1)S(1)}, bf16[512,256]{1,0:T(8,128)(2,1)}, u32[]{:S(2)}) copy-start(bf16[512,256]{1,0:T(8,128)(2,1)} %weight_ref.1) | copy-start | bytes 786436

commit v8 on v7

--- a/solution.py
+++ b/solution.py
@@ -88,12 +88,13 @@
     table = jnp.concatenate([table] * 4, axis=1).T[: table_ref.shape[1]].astype(i32)
     length = jnp.concatenate([length_ref[...].reshape(1, 32)] * 4, axis=1)
     start = page_size * lax.broadcasted_iota(i32, table.shape, 0)
-    inside = jnp.clip(length - start, 0, page_size).astype(f32)
-    rows = [
-        jnp.sum(jnp.where(table == first + page, inside, 0.0), axis=0, keepdims=True)
-        for page in range(pages)
-    ]
-    return jnp.concatenate(rows, axis=0).astype(i32)
+    inside = jnp.clip(length - start, 0, page_size)
+    page = first + lax.broadcasted_iota(i32, (pages, 128), 0)
+    count = jnp.zeros((pages, 128), i32)
+    for slot in range(table.shape[0]):
+        found = table[slot : slot + 1] == page
+        count = count + jnp.where(found, inside[slot : slot + 1], 0)
+    return count
 
 
 def regroup_queries(x_ref, out_ref):
@@ -138,18 +139,19 @@
     x = x_ref[...].astype(f32)
     tile = x[:, 32:40]
 
-    def column(place):
-        parts = [
-            sum(tile[:, :, 5 * (first + k) : 5 * (first + k) + 1] for k in range(3))
-            for first in range(place, 24, 6)
-        ]
-        return jnp.concatenate(parts, axis=1)
-
-    peaks, totals = column(0), column(3)
-    peak = jnp.max(peaks, axis=0)
-    factor = jnp.exp(peaks - peak[None])
-    outputs = jnp.sum(factor * x[:, 0:32], axis=0)
-    return outputs, peak, jnp.sum(factor * totals, axis=0)
+    members = tile.shape[0]
+    tile = tile.reshape(8 * members, 128)
+    tile = tile + pltpu.roll(tile, 123, 1) + pltpu.roll(tile, 118, 1)
+    tile = tile.reshape(members, 8, 128)
+    parts = []
+    for block in range(4):
+        lane = 30 * block
+        peaks = tile[:, :, lane : lane + 1]
+        peak = jnp.max(peaks, axis=0)
+        factor = jnp.exp(peaks - peak[None])
+        outputs = jnp.sum(factor * x[:, 8 * block : 8 * block + 8], axis=0)
+        parts.append((outputs, peak, jnp.sum(factor * tile[:, :, lane + 15 : lane + 16], axis=0)))
+    return tuple(jnp.concatenate(part, axis=0) for part in zip(*parts))
 
 
 def merge_near(x_ref, out_ref):

time: 88.2 us -> 88 us (level)
  no operation moved by 1% of the time
where the time goes in v8:
time: 88 us; the launch traced here: 87.5 us
  blocking collectives  54.4 us (62%)
  starting transfers between devices  27.7 us (31%)
  Pallas kernels  4.59 us (5%)
    all_to_all x4, blocking collectives, exchange(): lax.all_to_all(value, axes, split_axis=0, concat_axis=0, tiled=True, axis...  47.7 us
    all_to_all x1, starting transfers between devices, on_device(): lax.all_to_all(packed, KV, split_axis=0, concat_axis=0, tiled=True, axis_...  17 us
    ppermute x3, starting transfers between devices, on_device(): pieces[step] = lax.ppermute(pieces[step], 'y', ring)  10.7 us
    all_gather x1, blocking collectives, on_device(): attended = lax.all_gather(attended, NEAR)  6.67 us
    pallas_call x8, Pallas kernels, call(): pl.pallas_call(kernel, out_shape=out_shape, in_specs=[pl.BlockSpec(memory...  4.59 us
  transfers between devices with their start and end apart: 4, of which 0 were waited for; matrix products, arithmetic and copies ran while one was open for 0% of the time, Pallas kernels for 1%

profile of v8, /device:TPU:1, one launch (start us, length us, event | category | flops | bytes accessed | tf_op | source)
XLA Modules:
  0.0 87.5 jit_solution(9565341123738308362)
XLA Ops:
  0.0 0.7 copy-done.7
  0.7 0.7 queries_over_kv.1
  1.4 17.0 %all-to-all-start = ((bf16[32,4,128]{2,1,0:T(4,128)(2,1)}), bf16[32,4,128]{2,1,0:T(4,128)(2,1)S(1)}, u32[]{:S(2)}, u32[]{:S(2)}) async-start(bf16[32,4,128]{2,1,0:T(4,128)(2,1)} %queries_over_kv.1), calls=%async_computation | async-start | bytes 65536 | tf_op jit(solution)/shard_map/queries_over_kv/all_to_all | solution.py:266
  18.4 0.0 copy-done
  18.4 0.5 pages_over_y.1
  19.0 3.2 %collective-permute-start = (bf16[2,2,256,128]{3,2,1,0:T(8,128)(2,1)S(1)}, bf16[2,2,256,128]{3,2,1,0:T(8,128)(2,1)S(1)}, u32[]{:S(2)}, u32[]{:S(2)}) collective-permute-start(bf16[2,2,256,128]{3,2,1,0:T(8,128)(2,1)S(1)} %get-tuple-element.12), channel_id=1, source_target_pairs={{0,4},{4,8},{8,12},{12,0},{1,5},{5,9},{9,13},{13,1},{2,6},{6,10},{... | collective-permute-start | bytes 786440 | tf_op jit(solution)/shard_map/pages_over_y/ppermute | solution.py:280
  22.2 4.5 %collective-permute-start.1 = (bf16[2,2,256,128]{3,2,1,0:T(8,128)(2,1)S(1)}, bf16[2,2,256,128]{3,2,1,0:T(8,128)(2,1)S(1)}, u32[]{:S(2)}, u32[]{:S(2)}) collective-permute-start(bf16[2,2,256,128]{3,2,1,0:T(8,128)(2,1)S(1)} %get-tuple-element.13), channel_id=1, source_target_pairs={{0,8},{4,12},{8,0},{12,4},{1,9},{5,13},{9,1},{13,5},{2,10},{6,14},... | collective-permute-start | bytes 786440 | tf_op jit(solution)/shard_map/pages_over_y/ppermute | solution.py:280
  26.7 3.0 %collective-permute-start.2 = (bf16[2,2,256,128]{3,2,1,0:T(8,128)(2,1)S(1)}, bf16[2,2,256,128]{3,2,1,0:T(8,128)(2,1)S(1)}, u32[]{:S(2)}, u32[]{:S(2)}) collective-permute-start(bf16[2,2,256,128]{3,2,1,0:T(8,128)(2,1)S(1)} %get-tuple-element.14), channel_id=1, source_target_pairs={{0,12},{4,0},{8,4},{12,8},{1,13},{5,1},{9,5},{13,9},{2,14},{6,2},{... | collective-permute-start | bytes 786440 | tf_op jit(solution)/shard_map/pages_over_y/ppermute | solution.py:280
  29.7 0.0 all-to-all-done.x_ref
  29.7 0.1 queries_over_mp.1
  29.8 0.0 copy-start.4
  29.8 0.0 copy-start.5
  29.8 0.0 copy-start.6
  29.9 11.0 %all_to_all.25.refs_0_ = bf16[16,2,16,128]{3,2,1,0:T(8,128)(2,1)S(1)} all-to-all(bf16[16,2,16,128]{3,2,1,0:T(8,128)(2,1)S(1)} %queries_over_mp.1), channel_id=1, replica_groups=mesh['zo'=8,'zn'=2,'c'=2,'y'=4,'x'=4] {'y','x'}, dimensions={0} | all-to-all | bytes 262144 | tf_op jit(solution)/shard_map/queries_over_mp/all_to_all | solution.py:37
  40.9 0.0 collective-permute-done.refs_2_
  40.9 0.0 collective-permute-done.1.refs_3_
  40.9 0.0 collective-permute-done.2.refs_4_
  40.9 0.0 copy-done.4
  40.9 0.0 copy-done.5
  40.9 0.0 copy-done.6
  40.9 1.5 %attention.1 = (bf16[16,40,128]{2,1,0:T(8,128)(2,1)S(1)}, s32[32,128]{1,0:T(8,128)S(1)}) custom-call(bf16[16,2,16,128]{3,2,1,0:T(8,128)(2,1)S(1)} %all_to_all.25.refs_0_, bf16[2,2,256,128]{3,2,1,0:T(8,128)(2,1)S(1)} %get-tuple-element.11.refs_1_, bf16[2,2,256,128]{3,2,1,0:T(8,128)(2,1)S(1)} %collective-permute-done.refs_2_, ...), custom_call_target="tpu_custom_call" | custom-call | tf_op jit(solution)/shard_map/attention/pallas_call | solution.py:43
  42.4 12.5 %all_to_all.26.x_ref = bf16[16,40,128]{2,1,0:T(8,128)(2,1)S(1)} all-to-all(bf16[16,40,128]{2,1,0:T(8,128)(2,1)S(1)} %get-tuple-element.15), channel_id=1, replica_groups=mesh['zo'=8,'zn'=2,'c'=2,'y'=4,'x'=4] {'zn','c','x'}, dimensions={0} | all-to-all | bytes 327680 | tf_op jit(solution)/shard_map/merge/all_to_all | solution.py:37
  54.8 0.3 merge.2
  55.2 14.6 %all_to_all.27.x_ref = bf16[8,40,128]{2,1,0:T(8,128)(2,1)S(1)} all-to-all(bf16[8,40,128]{2,1,0:T(8,128)(2,1)S(1)} %merge.2), channel_id=1, replica_groups={{192,256,320,384,448,0,64,128},{193,257,321,385,449,1,65,129},{194,258,..., dimensions={0} | all-to-all | bytes 163840 | tf_op jit(solution)/shard_map/merge/all_to_all | solution.py:37
  69.8 0.3 merge.3
  70.1 6.7 %all-gather = bf16[128,128]{1,0:T(8,128)(2,1)S(1)} all-gather(bf16[32,128]{1,0:T(8,128)(2,1)S(1)} %merge.3), channel_id=2, replica_groups=mesh['zo'=8,'zn'=2,'c'=2,'y'=4,'x'=4] {'zn','c'}, dimensions={0}, use_global_device_ids=true | all-gather | bytes 40960 | tf_op jit(solution)/shard_map/merge/all_gather | solution.py:303
  76.8 0.0 copy-done.1
  76.8 0.0 copy-done.2
  76.8 0.0 copy-done.3
  76.8 0.5 projection.2
  77.3 9.6 %all_to_all.28.x_ref = bf16[16,4,128]{2,1,0:T(4,128)(2,1)S(1)} all-to-all(bf16[16,4,128]{2,1,0:T(4,128)(2,1)S(1)} %projection.2), channel_id=1, replica_groups=mesh['zo'=8,'zn'=2,'c'=2,'y'=4,'x'=4] {'y','x'}, dimensions={0} | all-to-all | bytes 32768 | tf_op jit(solution)/shard_map/projection/all_to_all | solution.py:37
  86.9 0.6 projection.3
  (5 shorter events, 0.0 us)
Async XLA Ops:
  0.0 0.7 copy-start.7
  0.7 17.7 %copy-start = (bf16[32,8,8,256]{3,2,1,0:T(8,128)(2,1)S(1)}, bf16[32,8,8,256]{3,2,1,0:T(8,128)(2,1)}, u32[]{:S(2)}) copy-start(bf16[32,8,8,256]{3,2,1,0:T(8,128)(2,1)} %kv_ref.1) | copy-start | bytes 3145732
  1.4 28.3 %all-to-all-start = ((bf16[32,4,128]{2,1,0:T(4,128)(2,1)}), bf16[32,4,128]{2,1,0:T(4,128)(2,1)S(1)}, u32[]{:S(2)}, u32[]{:S(2)}) async-start(bf16[32,4,128]{2,1,0:T(4,128)(2,1)} %queries_over_kv.1), calls=%async_computation | async-start | bytes 65536 | tf_op jit(solution)/shard_map/queries_over_kv/all_to_all | solution.py:266
  19.0 21.9 %collective-permute-start = (bf16[2,2,256,128]{3,2,1,0:T(8,128)(2,1)S(1)}, bf16[2,2,256,128]{3,2,1,0:T(8,128)(2,1)S(1)}, u32[]{:S(2)}, u32[]{:S(2)}) collective-permute-start(bf16[2,2,256,128]{3,2,1,0:T(8,128)(2,1)S(1)} %get-tuple-element.12), channel_id=1, source_target_pairs={{0,4},{4,8},{8,12},{12,0},{1,5},{5,9},{9,13},{13,1},{2,6},{6,10},{... | collective-permute-start | bytes 786440 | tf_op jit(solution)/shard_map/pages_over_y/ppermute | solution.py:280
  22.2 18.7 %collective-permute-start.1 = (bf16[2,2,256,128]{3,2,1,0:T(8,128)(2,1)S(1)}, bf16[2,2,256,128]{3,2,1,0:T(8,128)(2,1)S(1)}, u32[]{:S(2)}, u32[]{:S(2)}) collective-permute-start(bf16[2,2,256,128]{3,2,1,0:T(8,128)(2,1)S(1)} %get-tuple-element.13), channel_id=1, source_target_pairs={{0,8},{4,12},{8,0},{12,4},{1,9},{5,13},{9,1},{13,5},{2,10},{6,14},... | collective-permute-start | bytes 786440 | tf_op jit(solution)/shard_map/pages_over_y/ppermute | solution.py:280
  26.7 14.2 %collective-permute-start.2 = (bf16[2,2,256,128]{3,2,1,0:T(8,128)(2,1)S(1)}, bf16[2,2,256,128]{3,2,1,0:T(8,128)(2,1)S(1)}, u32[]{:S(2)}, u32[]{:S(2)}) collective-permute-start(bf16[2,2,256,128]{3,2,1,0:T(8,128)(2,1)S(1)} %get-tuple-element.14), channel_id=1, source_target_pairs={{0,12},{4,0},{8,4},{12,8},{1,13},{5,1},{9,5},{13,9},{2,14},{6,2},{... | collective-permute-start | bytes 786440 | tf_op jit(solution)/shard_map/pages_over_y/ppermute | solution.py:280
  29.8 11.1 %copy-start.4 = (s32[32,32]{1,0:T(8,128)S(1)}, s32[32,32]{1,0:T(8,128)}, u32[]{:S(2)}) copy-start(s32[32,32]{1,0:T(8,128)} %refs_5_.1) | copy-start | bytes 12292
  29.8 11.1 %copy-start.5 = (s32[32]{0:T(128)S(1)}, s32[32]{0:T(128)}, u32[]{:S(2)}) copy-start(s32[32]{0:T(128)} %refs_6_.1) | copy-start | bytes 388
  29.8 11.1 %copy-start.6 = (s32[32]{0:T(128)S(1)}, s32[32]{0:T(128)}, u32[]{:S(2)}) copy-start(s32[32]{0:T(128)} %refs_7_.1) | copy-start | bytes 388
  40.9 35.9 %copy-start.1 = (bf16[512,1024]{1,0:T(8,128)(2,1)S(1)}, bf16[512,1024]{1,0:T(8,128)(2,1)}, u32[]{:S(2)}) copy-start(bf16[512,1024]{1,0:T(8,128)(2,1)} %down_ref.1) | copy-start | bytes 3145732
  42.4 34.4 %copy-start.2 = (bf16[1024,256]{1,0:T(8,128)(2,1)S(1)}, bf16[1024,256]{1,0:T(8,128)(2,1)}, u32[]{:S(2)}) copy-start(bf16[1024,256]{1,0:T(8,128)(2,1)} %up_ref.1) | copy-start | bytes 1572868
  54.8 21.9 %copy-start.3 = (bf16[512,256]{1,0:T(8,128)(2,1)S(1)}, bf16[512,256]{1,0:T(8,128)(2,1)}, u32[]{:S(2)}) copy-start(bf16[512,256]{1,0:T(8,128)(2,1)} %weight_ref.1) | copy-start | bytes 786436

commit v9 on v8

--- a/solution.py
+++ b/solution.py
@@ -24,7 +24,7 @@
 i32 = jnp.int32
 
 
-QUERY_FIRST = 24
+QUERY_FIRST = 25
 MERGE_FIRST = 3
 QUERY_ORDER = sorted(
     range(32), key=lambda k: (k != QUERY_FIRST, abs((k - QUERY_FIRST + 16) % 32 - 16) // 2 * -1, k)

time: 88 us -> 87.7 us (level)
  no operation moved by 1% of the time
where the time goes in v9:
time: 87.7 us; the launch traced here: 87.2 us
  blocking collectives  54.4 us (62%)
  starting transfers between devices  27.4 us (31%)
  Pallas kernels  4.59 us (5%)
    all_to_all x4, blocking collectives, exchange(): lax.all_to_all(value, axes, split_axis=0, concat_axis=0, tiled=True, axis...  47.7 us
    all_to_all x1, starting transfers between devices, on_device(): lax.all_to_all(packed, KV, split_axis=0, concat_axis=0, tiled=True, axis_...  16.6 us
    ppermute x3, starting transfers between devices, on_device(): pieces[step] = lax.ppermute(pieces[step], 'y', ring)  10.7 us
    all_gather x1, blocking collectives, on_device(): attended = lax.all_gather(attended, NEAR)  6.67 us
    pallas_call x8, Pallas kernels, call(): pl.pallas_call(kernel, out_shape=out_shape, in_specs=[pl.BlockSpec(memory...  4.59 us
  transfers between devices with their start and end apart: 4, of which 0 were waited for; matrix products, arithmetic and copies ran while one was open for 0% of the time, Pallas kernels for 1%

profile of v9, /device:TPU:1, one launch (start us, length us, event | category | flops | bytes accessed | tf_op | source)
XLA Modules:
  0.0 87.2 jit_solution(4797858685878701166)
XLA Ops:
  0.0 0.7 copy-done.7
  0.7 0.7 queries_over_kv.1
  1.4 16.6 %all-to-all-start = ((bf16[32,4,128]{2,1,0:T(4,128)(2,1)}), bf16[32,4,128]{2,1,0:T(4,128)(2,1)S(1)}, u32[]{:S(2)}, u32[]{:S(2)}) async-start(bf16[32,4,128]{2,1,0:T(4,128)(2,1)} %queries_over_kv.1), calls=%async_computation | async-start | bytes 65536 | tf_op jit(solution)/shard_map/queries_over_kv/all_to_all | solution.py:266
  18.1 0.0 copy-done
  18.1 0.5 pages_over_y.1
  18.6 3.2 %collective-permute-start = (bf16[2,2,256,128]{3,2,1,0:T(8,128)(2,1)S(1)}, bf16[2,2,256,128]{3,2,1,0:T(8,128)(2,1)S(1)}, u32[]{:S(2)}, u32[]{:S(2)}) collective-permute-start(bf16[2,2,256,128]{3,2,1,0:T(8,128)(2,1)S(1)} %get-tuple-element.12), channel_id=1, source_target_pairs={{0,4},{4,8},{8,12},{12,0},{1,5},{5,9},{9,13},{13,1},{2,6},{6,10},{... | collective-permute-start | bytes 786440 | tf_op jit(solution)/shard_map/pages_over_y/ppermute | solution.py:280
  21.9 4.5 %collective-permute-start.1 = (bf16[2,2,256,128]{3,2,1,0:T(8,128)(2,1)S(1)}, bf16[2,2,256,128]{3,2,1,0:T(8,128)(2,1)S(1)}, u32[]{:S(2)}, u32[]{:S(2)}) collective-permute-start(bf16[2,2,256,128]{3,2,1,0:T(8,128)(2,1)S(1)} %get-tuple-element.13), channel_id=1, source_target_pairs={{0,8},{4,12},{8,0},{12,4},{1,9},{5,13},{9,1},{13,5},{2,10},{6,14},... | collective-permute-start | bytes 786440 | tf_op jit(solution)/shard_map/pages_over_y/ppermute | solution.py:280
  26.4 3.0 %collective-permute-start.2 = (bf16[2,2,256,128]{3,2,1,0:T(8,128)(2,1)S(1)}, bf16[2,2,256,128]{3,2,1,0:T(8,128)(2,1)S(1)}, u32[]{:S(2)}, u32[]{:S(2)}) collective-permute-start(bf16[2,2,256,128]{3,2,1,0:T(8,128)(2,1)S(1)} %get-tuple-element.14), channel_id=1, source_target_pairs={{0,12},{4,0},{8,4},{12,8},{1,13},{5,1},{9,5},{13,9},{2,14},{6,2},{... | collective-permute-start | bytes 786440 | tf_op jit(solution)/shard_map/pages_over_y/ppermute | solution.py:280
  29.4 0.0 all-to-all-done.x_ref
  29.4 0.1 queries_over_mp.1
  29.5 0.0 copy-start.4
  29.5 0.0 copy-start.5
  29.5 0.0 copy-start.6
  29.5 11.0 %all_to_all.25.refs_0_ = bf16[16,2,16,128]{3,2,1,0:T(8,128)(2,1)S(1)} all-to-all(bf16[16,2,16,128]{3,2,1,0:T(8,128)(2,1)S(1)} %queries_over_mp.1), channel_id=1, replica_groups=mesh['zo'=8,'zn'=2,'c'=2,'y'=4,'x'=4] {'y','x'}, dimensions={0} | all-to-all | bytes 262144 | tf_op jit(solution)/shard_map/queries_over_mp/all_to_all | solution.py:37
  40.5 0.0 collective-permute-done.refs_2_
  40.6 0.0 collective-permute-done.1.refs_3_
  40.6 0.0 collective-permute-done.2.refs_4_
  40.6 0.0 copy-done.4
  40.6 0.0 copy-done.5
  40.6 0.0 copy-done.6
  40.6 1.5 %attention.1 = (bf16[16,40,128]{2,1,0:T(8,128)(2,1)S(1)}, s32[32,128]{1,0:T(8,128)S(1)}) custom-call(bf16[16,2,16,128]{3,2,1,0:T(8,128)(2,1)S(1)} %all_to_all.25.refs_0_, bf16[2,2,256,128]{3,2,1,0:T(8,128)(2,1)S(1)} %get-tuple-element.11.refs_1_, bf16[2,2,256,128]{3,2,1,0:T(8,128)(2,1)S(1)} %collective-permute-done.refs_2_, ...), custom_call_target="tpu_custom_call" | custom-call | tf_op jit(solution)/shard_map/attention/pallas_call | solution.py:43
  42.1 12.5 %all_to_all.26.x_ref = bf16[16,40,128]{2,1,0:T(8,128)(2,1)S(1)} all-to-all(bf16[16,40,128]{2,1,0:T(8,128)(2,1)S(1)} %get-tuple-element.15), channel_id=1, replica_groups=mesh['zo'=8,'zn'=2,'c'=2,'y'=4,'x'=4] {'zn','c','x'}, dimensions={0} | all-to-all | bytes 327680 | tf_op jit(solution)/shard_map/merge/all_to_all | solution.py:37
  54.6 0.3 merge.2
  54.9 14.5 %all_to_all.27.x_ref = bf16[8,40,128]{2,1,0:T(8,128)(2,1)S(1)} all-to-all(bf16[8,40,128]{2,1,0:T(8,128)(2,1)S(1)} %merge.2), channel_id=1, replica_groups={{192,256,320,384,448,0,64,128},{193,257,321,385,449,1,65,129},{194,258,..., dimensions={0} | all-to-all | bytes 163840 | tf_op jit(solution)/shard_map/merge/all_to_all | solution.py:37
  69.4 0.3 merge.3
  69.7 6.7 %all-gather = bf16[128,128]{1,0:T(8,128)(2,1)S(1)} all-gather(bf16[32,128]{1,0:T(8,128)(2,1)S(1)} %merge.3), channel_id=2, replica_groups=mesh['zo'=8,'zn'=2,'c'=2,'y'=4,'x'=4] {'zn','c'}, dimensions={0}, use_global_device_ids=true | all-gather | bytes 40960 | tf_op jit(solution)/shard_map/merge/all_gather | solution.py:303
  76.4 0.0 copy-done.1
  76.4 0.0 copy-done.2
  76.4 0.0 copy-done.3
  76.4 0.5 projection.2
  76.9 9.7 %all_to_all.28.x_ref = bf16[16,4,128]{2,1,0:T(4,128)(2,1)S(1)} all-to-all(bf16[16,4,128]{2,1,0:T(4,128)(2,1)S(1)} %projection.2), channel_id=1, replica_groups=mesh['zo'=8,'zn'=2,'c'=2,'y'=4,'x'=4] {'y','x'}, dimensions={0} | all-to-all | bytes 32768 | tf_op jit(solution)/shard_map/projection/all_to_all | solution.py:37
  86.6 0.6 projection.3
  (5 shorter events, 0.0 us)
Async XLA Ops:
  0.0 0.7 copy-start.7
  0.7 17.4 %copy-start = (bf16[32,8,8,256]{3,2,1,0:T(8,128)(2,1)S(1)}, bf16[32,8,8,256]{3,2,1,0:T(8,128)(2,1)}, u32[]{:S(2)}) copy-start(bf16[32,8,8,256]{3,2,1,0:T(8,128)(2,1)} %kv_ref.1) | copy-start | bytes 3145732
  1.4 27.9 %all-to-all-start = ((bf16[32,4,128]{2,1,0:T(4,128)(2,1)}), bf16[32,4,128]{2,1,0:T(4,128)(2,1)S(1)}, u32[]{:S(2)}, u32[]{:S(2)}) async-start(bf16[32,4,128]{2,1,0:T(4,128)(2,1)} %queries_over_kv.1), calls=%async_computation | async-start | bytes 65536 | tf_op jit(solution)/shard_map/queries_over_kv/all_to_all | solution.py:266
  18.6 21.9 %collective-permute-start = (bf16[2,2,256,128]{3,2,1,0:T(8,128)(2,1)S(1)}, bf16[2,2,256,128]{3,2,1,0:T(8,128)(2,1)S(1)}, u32[]{:S(2)}, u32[]{:S(2)}) collective-permute-start(bf16[2,2,256,128]{3,2,1,0:T(8,128)(2,1)S(1)} %get-tuple-element.12), channel_id=1, source_target_pairs={{0,4},{4,8},{8,12},{12,0},{1,5},{5,9},{9,13},{13,1},{2,6},{6,10},{... | collective-permute-start | bytes 786440 | tf_op jit(solution)/shard_map/pages_over_y/ppermute | solution.py:280
  21.9 18.7 %collective-permute-start.1 = (bf16[2,2,256,128]{3,2,1,0:T(8,128)(2,1)S(1)}, bf16[2,2,256,128]{3,2,1,0:T(8,128)(2,1)S(1)}, u32[]{:S(2)}, u32[]{:S(2)}) collective-permute-start(bf16[2,2,256,128]{3,2,1,0:T(8,128)(2,1)S(1)} %get-tuple-element.13), channel_id=1, source_target_pairs={{0,8},{4,12},{8,0},{12,4},{1,9},{5,13},{9,1},{13,5},{2,10},{6,14},... | collective-permute-start | bytes 786440 | tf_op jit(solution)/shard_map/pages_over_y/ppermute | solution.py:280
  26.4 14.2 %collective-permute-start.2 = (bf16[2,2,256,128]{3,2,1,0:T(8,128)(2,1)S(1)}, bf16[2,2,256,128]{3,2,1,0:T(8,128)(2,1)S(1)}, u32[]{:S(2)}, u32[]{:S(2)}) collective-permute-start(bf16[2,2,256,128]{3,2,1,0:T(8,128)(2,1)S(1)} %get-tuple-element.14), channel_id=1, source_target_pairs={{0,12},{4,0},{8,4},{12,8},{1,13},{5,1},{9,5},{13,9},{2,14},{6,2},{... | collective-permute-start | bytes 786440 | tf_op jit(solution)/shard_map/pages_over_y/ppermute | solution.py:280
  29.5 11.1 %copy-start.4 = (s32[32,32]{1,0:T(8,128)S(1)}, s32[32,32]{1,0:T(8,128)}, u32[]{:S(2)}) copy-start(s32[32,32]{1,0:T(8,128)} %refs_5_.1) | copy-start | bytes 12292
  29.5 11.1 %copy-start.5 = (s32[32]{0:T(128)S(1)}, s32[32]{0:T(128)}, u32[]{:S(2)}) copy-start(s32[32]{0:T(128)} %refs_6_.1) | copy-start | bytes 388
  29.5 11.1 %copy-start.6 = (s32[32]{0:T(128)S(1)}, s32[32]{0:T(128)}, u32[]{:S(2)}) copy-start(s32[32]{0:T(128)} %refs_7_.1) | copy-start | bytes 388
  40.5 35.8 %copy-start.1 = (bf16[512,1024]{1,0:T(8,128)(2,1)S(1)}, bf16[512,1024]{1,0:T(8,128)(2,1)}, u32[]{:S(2)}) copy-start(bf16[512,1024]{1,0:T(8,128)(2,1)} %down_ref.1) | copy-start | bytes 3145732
  42.1 34.3 %copy-start.2 = (bf16[1024,256]{1,0:T(8,128)(2,1)S(1)}, bf16[1024,256]{1,0:T(8,128)(2,1)}, u32[]{:S(2)}) copy-start(bf16[1024,256]{1,0:T(8,128)(2,1)} %up_ref.1) | copy-start | bytes 1572868
  54.6 21.8 %copy-start.3 = (bf16[512,256]{1,0:T(8,128)(2,1)S(1)}, bf16[512,256]{1,0:T(8,128)(2,1)}, u32[]{:S(2)}) copy-start(bf16[512,256]{1,0:T(8,128)(2,1)} %weight_ref.1) | copy-start | bytes 786436
